TPU v7x, 32 devices: a whole 2x2x4 slice. The times are simulated.
32 devices in a mesh: tok: 16 (over z, y, x), atm: 2 (over core).
Axes of the slice: x: 2, y: 2, z: 4, core: 2. Of those that a mesh axis runs over, the one named last changes fastest.
Arguments:
- pair: bfloat16 [448, 448, 128], P('tok'), may hold values from -6 to 6
- tri_in: bfloat16 [4, 128, 128], replicated, may hold values from -0.5 to 0.5
- tri_gate: bfloat16 [128, 128], replicated, may hold values from -0.5 to 0.5
- tri_out: bfloat16 [128, 128], replicated, may hold values from -0.5 to 0.5
- pair_proj: bfloat16 [128, 16], replicated, may hold values from -0.5 to 0.5
- atom_act: bfloat16 [4096, 128], P(('tok', 'atm')), may hold values from -6 to 6
- atom_cond: bfloat16 [4096, 128], P(('tok', 'atm')), may hold values from -72 to 72
- cond_pair: bfloat16 [2, 128, 16], replicated, may hold values from -0.5 to 0.5
- pair_mlp: bfloat16 [16, 16], replicated, may hold values from -1.5 to 1.5
- bias_proj: bfloat16 [3, 16, 4], replicated, may hold values from -1.5 to 1.5
- block_weights: bfloat16 [3, 7, 128, 128], replicated, may hold values from -0.5 to 0.5
- atom_token: int32 [4096], P(('tok', 'atm')), may hold values from 0 to 447, as said below
- atom_mask: int32 [4096], P(('tok', 'atm')), may hold values from 0 to 1, as said below
- key_start: int32 [128], P(('tok', 'atm')), may hold values from 0 to 3968, as said below
- key_tiles: int32 [128, 40], P(('tok', 'atm')), may hold values from -1 to 447, as said below
Outputs:
- pair_band: bfloat16 [448, 84, 128], P('tok')
- atoms_out: bfloat16 [4096, 128], P(('tok', 'atm'))
Inputs may be any that keep to these rules, and one draw needn't show every extreme that they name: `atom_token`: Nondecreasing; atoms 2 * 128 * s to 2 * 128 * s + 2 * 128 - 1 belong to tokens 28 * s to 28 * s + 27, and every token owns 4 atoms or more. `atom_mask`: each token's first atom is valid. key_start[w] is 32 * w - 48 moved by at most 16, clipped to the atoms' range. `key_tiles`: row w lists, rising by one, every token that owns one of window w's key atoms, then -1 in the remaining slots.
All inputs are finite; a program needn't handle non-finite values.
Results may differ from a plain program's by a relative error of at most 0.013.
Values may be sent and summed in bfloat16 or wider, within the bound.
A program may use at most 256 MiB of HBM per device.

v0:
```python
import jax
import jax.numpy as jnp
from jax import lax
from jax.sharding import PartitionSpec as P

QUERY_ATOMS = 32
KW = 128
HALO = 64
BLOCKS = 3


def with_halo(x, sides, width):
    for axis, dim in sides:
        peers, length = (lax.axis_size(axis), x.shape[dim])
        up = [(i, (i + 1) % peers) for i in range(peers - 1)]
        down = [(j, i) for i, j in up]
        last = lax.slice_in_dim(x, length - width, length, axis=dim)
        leading = lax.slice_in_dim(x, 0, width, axis=dim)
        before = lax.ppermute(last, axis, up)
        after = lax.ppermute(leading, axis, down)
        x = jnp.concatenate([before, x, after], axis=dim)
    return x


def normalize(values):
    values = values.astype(jnp.float32)
    centred = values - jnp.mean(values, -1, keepdims=True)
    return centred * lax.rsqrt(jnp.mean(centred * centred, -1, keepdims=True) + 1e-05)


def project_rows(rows, tri_in):

    def one_row(row):
        normed = normalize(row).astype(jnp.bfloat16)
        parts = [
            jnp.dot(normed, tri_in[which], preferred_element_type=jnp.float32) for which in range(4)
        ]
        left = (jax.nn.sigmoid(parts[0]) * parts[1]).astype(jnp.bfloat16)
        right = (jax.nn.sigmoid(parts[2]) * parts[3]).astype(jnp.bfloat16)
        return (left, right)

    return lax.map(one_row, rows)


def local(
    pair,
    tri_in,
    tri_gate,
    tri_out,
    pair_proj,
    atom_act,
    atom_cond,
    cond_pair,
    pair_mlp,
    bias_proj,
    block_weights,
    atom_token,
    atom_mask,
    key_start,
    key_tiles,
):
    tok_dev = pair.shape[0]
    shard = lax.axis_index("tok")
    left, right = project_rows(pair, tri_in)
    beside_all = with_halo(right, (("tok", 0),), tok_dev)
    prod = jnp.einsum("ikc,jkc->ijc", left, beside_all, preferred_element_type=jnp.float32)
    padded = jnp.pad(pair, ((0, 0), (tok_dev, tok_dev), (0, 0)))
    band = lax.dynamic_slice_in_dim(padded, shard * tok_dev, 3 * tok_dev, 1)
    gate = jax.nn.sigmoid(
        jnp.dot(normalize(band).astype(jnp.bfloat16), tri_gate, preferred_element_type=jnp.float32)
    )
    update = jnp.dot(
        normalize(prod).astype(jnp.bfloat16), tri_out, preferred_element_type=jnp.float32
    )
    pair_band = (band.astype(jnp.float32) + gate * update).astype(jnp.bfloat16)
    pair_tok = jnp.dot(
        normalize(pair_band).astype(jnp.bfloat16), pair_proj, preferred_element_type=jnp.float32
    ).astype(jnp.bfloat16)
    atoms = atom_act.shape[0]
    width = atom_act.shape[1]
    windows = key_start.shape[0]
    heads = bias_proj.shape[2]
    head_dim = width // heads
    device = shard * lax.axis_size("atm") + lax.axis_index("atm")
    first_atom = device * atoms
    labels = jnp.stack([atom_token, atom_mask], 1)
    labels_ext = with_halo(labels, ((("tok", "atm"), 0),), HALO)
    relu_cond = jax.nn.relu(atom_cond)
    query_term = jnp.dot(relu_cond, cond_pair[0], preferred_element_type=jnp.float32)
    key_term = jnp.dot(relu_cond, cond_pair[1], preferred_element_type=jnp.float32)
    key_term_ext = with_halo(key_term, ((("tok", "atm"), 0),), HALO)
    offsets = key_start - first_atom + HALO
    mlp_weight = pair_mlp.astype(jnp.float32)
    row_slots = jnp.arange(tok_dev, dtype=jnp.int32)
    band_slots = jnp.arange(3 * tok_dev, dtype=jnp.int32)

    def window_pair(offset, tiles, query_tokens, window_queries):
        key_labels = lax.dynamic_slice_in_dim(labels_ext, offset, KW, 0)
        key_rows = lax.dynamic_slice_in_dim(key_term_ext, offset, KW, 0)
        rows_hot = (query_tokens[:, None] - shard * tok_dev == row_slots[None, :]).astype(
            jnp.bfloat16
        )
        picked = jnp.einsum(
            "li,ijc->ljc", rows_hot, pair_tok, preferred_element_type=jnp.float32
        ).astype(jnp.bfloat16)
        live = tiles >= 0
        cols_hot = jnp.logical_and(
            tiles[:, None] - (shard - 1) * tok_dev == band_slots[None, :], live[:, None]
        ).astype(jnp.bfloat16)
        tiled = jnp.einsum(
            "ljc,rj->lrc", picked, cols_hot, preferred_element_type=jnp.float32
        ).astype(jnp.bfloat16)
        keys_hot = jnp.logical_and(key_labels[:, 0:1] == tiles[None, :], live[None, :]).astype(
            jnp.bfloat16
        )
        selected = jnp.einsum("lrc,mr->lmc", tiled, keys_hot, preferred_element_type=jnp.float32)
        pbase = selected + window_queries[:, None, :] + key_rows[None, :, :]
        refined = pbase + jnp.einsum(
            "lmc,cd->lmd", jax.nn.relu(pbase), mlp_weight, precision=lax.Precision.HIGHEST
        )
        return (refined, key_labels[:, 1])

    refined, key_valid = jax.vmap(window_pair)(
        offsets,
        key_tiles,
        atom_token.reshape(windows, QUERY_ATOMS),
        query_term.reshape(windows, QUERY_ATOMS, -1),
    )
    cond_normed = normalize(atom_cond).astype(jnp.bfloat16)
    state = atom_act.astype(jnp.float32)
    for block in range(BLOCKS):
        layer = block_weights[block]
        bias = jnp.einsum(
            "wlmc,ch->whlm",
            refined,
            bias_proj[block].astype(jnp.float32),
            precision=lax.Precision.HIGHEST,
        )
        scale_gate = jax.nn.sigmoid(
            jnp.dot(cond_normed, layer[0], preferred_element_type=jnp.float32)
        )
        shifted = jnp.dot(cond_normed, layer[1], preferred_element_type=jnp.float32)
        normed = (scale_gate * normalize(state) + shifted).astype(jnp.bfloat16)
        queries = (
            jnp.dot(normed, layer[2], preferred_element_type=jnp.float32) * head_dim ** (-0.5)
        ).astype(jnp.bfloat16)
        gates = jax.nn.sigmoid(jnp.dot(normed, layer[5], preferred_element_type=jnp.float32))
        normed_ext = with_halo(normed, ((("tok", "atm"), 0),), HALO)
        keys_all = jnp.dot(normed_ext, layer[3], preferred_element_type=jnp.float32).astype(
            jnp.bfloat16
        )
        values_all = jnp.dot(normed_ext, layer[4], preferred_element_type=jnp.float32).astype(
            jnp.bfloat16
        )

        def attend(offset, window_queries, pair_bias_rows, valid):
            windowed_key_rows = lax.dynamic_slice_in_dim(keys_all, offset, KW, 0).reshape(
                KW, heads, head_dim
            )
            windowed_value_rows = lax.dynamic_slice_in_dim(values_all, offset, KW, 0).reshape(
                KW, heads, head_dim
            )
            attention_logits = (
                jnp.einsum(
                    "fqy,uqy->qfu",
                    window_queries.reshape(QUERY_ATOMS, heads, head_dim),
                    windowed_key_rows,
                    preferred_element_type=jnp.float32,
                )
                + pair_bias_rows
            )
            attention_logits = jnp.where(
                valid[None, None, :] > 0, attention_logits, jnp.float32(-1e30)
            )
            attention_weights = jax.nn.softmax(attention_logits, -1).astype(jnp.bfloat16)
            blended_output = jnp.einsum(
                "bwv,vbi->wbi",
                attention_weights,
                windowed_value_rows,
                preferred_element_type=jnp.float32,
            )
            return blended_output.reshape(QUERY_ATOMS, width)

        blended_output = jax.vmap(attend)(
            offsets, queries.reshape(windows, QUERY_ATOMS, width), bias, key_valid
        ).reshape(atoms, width)
        attended = (blended_output * gates).astype(jnp.bfloat16)
        state = state + jnp.dot(attended, layer[6], preferred_element_type=jnp.float32)
    return (pair_band, state.astype(jnp.bfloat16))


def solution(mesh):
    in_specs = (
        P("tok", None, None),
        P(),
        P(),
        P(),
        P(),
        P(("tok", "atm"), None),
        P(("tok", "atm"), None),
        P(),
        P(),
        P(),
        P(),
        P(("tok", "atm")),
        P(("tok", "atm")),
        P(("tok", "atm")),
        P(("tok", "atm"), None),
    )
    out_specs = (P("tok", None, None), P(("tok", "atm"), None))
    return jax.shard_map(local, mesh=mesh, in_specs=in_specs, out_specs=out_specs, check_vma=False)
```

profile of v0, /device:TPU:23, one launch (start us, length us, event | category | flops | bytes accessed | tf_op | source)
XLA Modules:
  0.0 507.3 jit_solution(17089060064680322720)
XLA Ops:
  0.7 234.1 %while.20 = (s32[]{:T(128)}, bf16[28,448,128]{2,1,0:T(8,128)(2,1)}, bf16[28,448,128]{2,1,0:T(8,128)(2,1)}, bf16[28,448,128]{2,1,0:T(8,128)(2,1)}, bf16[4,128,128]{2,1,0:T(8,128)(2,1)}, /*index=5*/s32[]{:T(128)}) while((s32[]{:T(128)}, bf16[28,448,128]{2,1,0:T(8,128)(2,1)}, bf16[28,448,128]{2,1,0:T(8,128)(2,1)}, ...), condition=%wide.region_5.6_spmd, body=%wide.region_2.5_spmd.sunk | while | flops 60555712 | bytes 1996109 | solution.py:42
  7.2 1.9 fusion.290
  12.5 1.9 fusion.292
  20.9 1.9 fusion.292
  40.6 1.9 fusion.290
  62.6 1.9 fusion.292
  65.7 1.9 fusion.290
  71.0 1.9 fusion.292
  74.1 1.9 fusion.290
  90.8 1.9 fusion.290
  104.5 1.9 fusion.292
  129.5 1.9 fusion.292
  162.9 1.9 fusion.292
  171.3 1.9 fusion.292
  174.4 1.9 fusion.290
  188.0 1.9 fusion.292
  191.1 1.9 fusion.290
  196.4 1.9 fusion.292
  199.5 1.9 fusion.290
  234.8 3.1 collective-permute-start
  237.9 2.2 collective-permute-start.1
  240.8 6.0 %collective-permute-start.4 = (s32[64,2]{0,1:T(2,128)}, s32[64,2]{0,1:T(2,128)}, u32[]{:S(2)}, u32[]{:S(2)}) collective-permute-start(s32[64,2]{0,1:T(2,128)} %get-tuple-element.178), channel_id=1, source_target_pairs={{0,1},{1,2},{2,3},{3,4},{4,5},{5,6},{6,7},{7,8},{8,9},{9,10},{10,1... | collective-permute-start | bytes 1544 | tf_op jit(solution)/shard_map/ppermute | solution.py:19
  246.8 1.9 collective-permute-start.5
  249.6 5.4 %collective-permute-start.6 = (f32[64,16]{0,1:T(8,128)}, f32[64,16]{0,1:T(8,128)S(1)}, u32[]{:S(2)}, u32[]{:S(2)}) collective-permute-start(f32[64,16]{0,1:T(8,128)} %get-tuple-element.176), channel_id=1, source_target_pairs={{0,1},{1,2},{2,3},{3,4},{4,5},{5,6},{6,7},{7,8},{8,9},{9,10},{10,1... | collective-permute-start | bytes 12296 | tf_op jit(solution)/shard_map/ppermute | solution.py:19
  255.0 7.9 %copy.70 = bf16[28,448,128]{1,0,2:T(8,128)(2,1)} copy(bf16[28,448,128]{2,1,0:T(8,128)(2,1)} %get-tuple-element.30) | data formatting | bytes 6422528 | tf_op jit(solution)/shard_map/while | solution.py:42
  269.8 1.9 fusion.45
  271.8 7.8 %copy.72 = bf16[28,448,128]{1,0,2:T(8,128)(2,1)} copy(bf16[28,448,128]{2,1,0:T(8,128)(2,1)} %get-tuple-element.31) | data formatting | bytes 6422528 | tf_op jit(solution)/shard_map/while | solution.py:42
  279.8 26.6 %collective-permute-done.4 = s32[64,2]{0,1:T(2,128)} collective-permute-done((s32[64,2]{0,1:T(2,128)}, s32[64,2]{0,1:T(2,128)}, u32[]{:S(2)}, u32[]{:S(2)}) %collective-permute-start.4) | collective-permute-done | bytes 544 | tf_op jit(solution)/shard_map/ppermute | solution.py:19
  306.4 71.9 %collective-permute-start.7 = (f32[64,16]{0,1:T(8,128)S(1)}, f32[64,16]{0,1:T(8,128)S(1)}, u32[]{:S(2)}, u32[]{:S(2)}) collective-permute-start(f32[64,16]{0,1:T(8,128)S(1)} %copy-done.17), channel_id=1, source_target_pairs={{1,0},{2,1},{3,2},{4,3},{5,4},{6,5},{7,6},{8,7},{9,8},{10,9},{11,1... | collective-permute-start | bytes 12296 | tf_op jit(solution)/shard_map/ppermute | solution.py:20
  378.4 1.9 collective-permute-start.2
  381.1 5.5 %while.22 = (s32[]{:T(128)}, s32[256,2]{0,1:T(2,128)S(1)}, s32[4,2]{0,1:T(2,128)S(1)}, s32[4,128,2]{1,2,0:T(2,128)S(1)}, s32[]{:T(128)}) while((s32[]{:T(128)}, s32[256,2]{0,1:T(2,128)S(1)}, s32[4,2]{0,1:T(2,128)S(1)}, s32[4,128,2]{1,2,0:T(2,128)S(1)}, s32[]{:T(128)}) %tuple.154), condition=%wide.while_cond.1, body=%wide.while_body.1.sunk | while | flops 2 | bytes 2145 | solution.py:98
  387.7 2.4 collective-permute-start.3
  390.2 7.6 %while.24 = (s32[]{:T(128)}, f32[256,16]{0,1:T(8,128)S(1)}, s32[4,2]{0,1:T(2,128)S(1)}, f32[4,128,16]{1,2,0:T(8,128)}, s32[]{:T(128)}) while((s32[]{:T(128)}, f32[256,16]{0,1:T(8,128)S(1)}, s32[4,2]{0,1:T(2,128)S(1)}, f32[4,128,16]{1,2,0:T(8,128)}, s32[]{:T(128)}) %tuple.147), condition=%wide.while_cond.3, body=%wide.while_body.3.sunk | while | flops 2 | bytes 17497 | solution.py:99
  401.0 11.1 %while.23 = (s32[]{:T(128)}, bf16[256,128]{1,0:T(8,128)(2,1)}, s32[4,2]{0,1:T(2,128)S(1)}, bf16[4,128,128]{1,2,0:T(8,128)(2,1)}, s32[]{:T(128)}) while((s32[]{:T(128)}, bf16[256,128]{1,0:T(8,128)(2,1)}, s32[4,2]{0,1:T(2,128)S(1)}, bf16[4,128,128]{1,2,0:T(8,128)(2,1)}, s32[]{:T(128)}) %tuple.148), condition=%wide.while_cond.2, body=%wide.while_body.2.sunk | while | flops 2 | bytes 197213 | solution.py:157
  412.8 8.0 %while.21 = (s32[]{:T(128)}, bf16[256,128]{1,0:T(8,128)(2,1)S(1)}, s32[4,2]{0,1:T(2,128)S(1)}, bf16[4,128,128]{1,2,0:T(8,128)(2,1)}, s32[]{:T(128)}) while((s32[]{:T(128)}, bf16[256,128]{1,0:T(8,128)(2,1)S(1)}, s32[4,2]{0,1:T(2,128)S(1)}, bf16[4,128,128]{1,2,0:T(8,128)(2,1)}, s32[]{:T(128)}) %tuple.149), condition=%wide.while_cond, body=%wide.while_body.sunk | while | flops 2 | bytes 197213 | solution.py:160
  420.8 7.8 %copy.69 = bf16[28,448,128]{1,0,2:T(8,128)(2,1)} copy(bf16[28,448,128]{2,1,0:T(8,128)(2,1)} %collective-permute-done) | data formatting | bytes 6422528 | tf_op jit(solution)/shard_map/ppermute | solution.py:19
  428.5 7.8 %copy.71 = bf16[28,448,128]{1,0,2:T(8,128)(2,1)} copy(bf16[28,448,128]{2,1,0:T(8,128)(2,1)} %collective-permute-done.1) | data formatting | bytes 6422528 | tf_op jit(solution)/shard_map/ppermute | solution.py:20
  436.3 8.1 %bitcast_reduce_fusion = (f32[28,84]{1,0:T(8,128)S(1)}, f32[128,84,28]{1,2,0:T(8,128)S(1)}) fusion(bf16[28,448,128]{1,0,2:T(8,128)(2,1)} %copy.72, bf16[28,448,128]{1,0,2:T(8,128)(2,1)} %copy.71, bf16[28,448,128]{1,0,2:T(8,128)(2,1)} %copy.70, bf16[28,448,128]{1,0,2:T(8,128)(2,1)} %copy.69), kind=kOutput, calls=%fused_computation.68 | convolution fusion | flops 298946240 | bytes 14058688 | tf_op jit(solution)/shard_map/ikc,jkc->ijc/dot_general | solution.py:66
  458.1 5.0 collective-permute-start.8
  463.0 1.9 collective-permute-start.9
  465.2 4.7 collective-permute-done.9
  470.1 5.6 %while.26 = (s32[]{:T(128)}, bf16[256,128]{1,0:T(8,128)(2,1)S(1)}, s32[4,2]{0,1:T(2,128)S(1)}, bf16[4,128,128]{1,2,0:T(8,128)(2,1)S(1)}, s32[]{:T(128)}) while((s32[]{:T(128)}, bf16[256,128]{1,0:T(8,128)(2,1)S(1)}, s32[4,2]{0,1:T(2,128)S(1)}, bf16[4,128,128]{1,2,0:T(8,128)(2,1)S(1)}, s32[]{:T(128)}) %tuple.150), condition=%wide.while_cond.5, body=%wide.while_body.5.sunk | while | flops 2 | bytes 196705 | solution.py:157
  476.3 5.6 %while.25 = (s32[]{:T(128)}, bf16[256,128]{1,0:T(8,128)(2,1)S(1)}, s32[4,2]{0,1:T(2,128)S(1)}, bf16[4,128,128]{1,2,0:T(8,128)(2,1)S(1)}, s32[]{:T(128)}) while((s32[]{:T(128)}, bf16[256,128]{1,0:T(8,128)(2,1)S(1)}, s32[4,2]{0,1:T(2,128)S(1)}, bf16[4,128,128]{1,2,0:T(8,128)(2,1)S(1)}, s32[]{:T(128)}) %tuple.151), condition=%wide.while_cond.4, body=%wide.while_body.4.sunk | while | flops 2 | bytes 196705 | solution.py:160
  484.3 1.9 collective-permute-start.10
  486.2 2.4 collective-permute-start.11
  488.9 4.2 collective-permute-done.11
  493.2 5.6 %while.28 = (s32[]{:T(128)}, bf16[256,128]{1,0:T(8,128)(2,1)S(1)}, s32[4,2]{0,1:T(2,128)S(1)}, bf16[4,128,128]{1,2,0:T(8,128)(2,1)S(1)}, s32[]{:T(128)}) while((s32[]{:T(128)}, bf16[256,128]{1,0:T(8,128)(2,1)S(1)}, s32[4,2]{0,1:T(2,128)S(1)}, bf16[4,128,128]{1,2,0:T(8,128)(2,1)S(1)}, s32[]{:T(128)}) %tuple.152), condition=%wide.while_cond.7, body=%wide.while_body.7.sunk | while | flops 2 | bytes 196705 | solution.py:157
  499.5 5.6 %while.27 = (s32[]{:T(128)}, bf16[256,128]{1,0:T(8,128)(2,1)S(1)}, s32[4,2]{0,1:T(2,128)S(1)}, bf16[4,128,128]{1,2,0:T(8,128)(2,1)S(1)}, s32[]{:T(128)}) while((s32[]{:T(128)}, bf16[256,128]{1,0:T(8,128)(2,1)S(1)}, s32[4,2]{0,1:T(2,128)S(1)}, bf16[4,128,128]{1,2,0:T(8,128)(2,1)S(1)}, s32[]{:T(128)}) %tuple.153), condition=%wide.while_cond.6, body=%wide.while_body.6.sunk | while | flops 2 | bytes 196705 | solution.py:160
  (523 shorter events, 287.9 us)
Async XLA Ops:
  0.6 444.5 %copy-start = (bf16[128,128]{1,0:T(8,128)(2,1)S(1)}, bf16[128,128]{1,0:T(8,128)(2,1)}, u32[]{:S(2)}) copy-start(bf16[128,128]{1,0:T(8,128)(2,1)} %param.20) | copy-start | bytes 98308
  0.7 239.4 %copy-start.26 = (s32[128]{0:T(128)S(1)}, s32[128]{0:T(128)}, u32[]{:S(2)}) copy-start(s32[128]{0:T(128)} %param.28) | copy-start | bytes 1540
  0.7 239.4 %copy-start.28 = (s32[128]{0:T(128)S(1)}, s32[128]{0:T(128)}, u32[]{:S(2)}) copy-start(s32[128]{0:T(128)} %param.29) | copy-start | bytes 1540
  0.7 248.0 %copy-start.3 = (bf16[128,128]{1,0:T(8,128)(2,1)S(1)}, bf16[128,128]{1,0:T(8,128)(2,1)}, u32[]{:S(2)}) copy-start(bf16[128,128]{1,0:T(8,128)(2,1)} %param.23) | copy-start | bytes 98308
  0.7 248.0 %copy-start.16 = (bf16[2,128,16]{1,2,0:T(8,128)(2,1)S(1)}, bf16[2,128,16]{1,2,0:T(8,128)(2,1)}, u32[]{:S(2)}) copy-start(bf16[2,128,16]{1,2,0:T(8,128)(2,1)} %param.24) | copy-start | bytes 24580
  234.8 186.0 %collective-permute-start = (bf16[28,448,128]{2,1,0:T(8,128)(2,1)}, bf16[28,448,128]{2,1,0:T(8,128)(2,1)}, u32[]{:S(2)}, u32[]{:S(2)}) collective-permute-start(bf16[28,448,128]{2,1,0:T(8,128)(2,1)} %get-tuple-element.30), channel_id=1, source_target_pairs={{0,2},{2,4},{4,6},{6,8},{8,10},{10,12},{12,14},{14,16},{16,18},{18... | collective-permute-start | bytes 9633800 | tf_op jit(solution)/shard_map/ppermute | solution.py:19
  237.9 190.6 %collective-permute-start.1 = (bf16[28,448,128]{2,1,0:T(8,128)(2,1)}, bf16[28,448,128]{2,1,0:T(8,128)(2,1)}, u32[]{:S(2)}, u32[]{:S(2)}) collective-permute-start(bf16[28,448,128]{2,1,0:T(8,128)(2,1)} %get-tuple-element.30), channel_id=1, source_target_pairs={{2,0},{4,2},{6,4},{8,6},{10,8},{12,10},{14,12},{16,14},{18,16},{20... | collective-permute-start | bytes 9633800 | tf_op jit(solution)/shard_map/ppermute | solution.py:20
  240.8 65.7 %collective-permute-start.4 = (s32[64,2]{0,1:T(2,128)}, s32[64,2]{0,1:T(2,128)}, u32[]{:S(2)}, u32[]{:S(2)}) collective-permute-start(s32[64,2]{0,1:T(2,128)} %get-tuple-element.178), channel_id=1, source_target_pairs={{0,1},{1,2},{2,3},{3,4},{4,5},{5,6},{6,7},{7,8},{8,9},{9,10},{10,1... | collective-permute-start | bytes 1544 | tf_op jit(solution)/shard_map/ppermute | solution.py:19
  246.8 131.6 %collective-permute-start.5 = (s32[64,2]{0,1:T(2,128)}, s32[64,2]{0,1:T(2,128)}, u32[]{:S(2)}, u32[]{:S(2)}) collective-permute-start(s32[64,2]{0,1:T(2,128)} %get-tuple-element.179), channel_id=1, source_target_pairs={{1,0},{2,1},{3,2},{4,3},{5,4},{6,5},{7,6},{8,7},{9,8},{10,9},{11,1... | collective-permute-start | bytes 1544 | tf_op jit(solution)/shard_map/ppermute | solution.py:20
  249.6 138.1 %collective-permute-start.6 = (f32[64,16]{0,1:T(8,128)}, f32[64,16]{0,1:T(8,128)S(1)}, u32[]{:S(2)}, u32[]{:S(2)}) collective-permute-start(f32[64,16]{0,1:T(8,128)} %get-tuple-element.176), channel_id=1, source_target_pairs={{0,1},{1,2},{2,3},{3,4},{4,5},{5,6},{6,7},{7,8},{8,9},{9,10},{10,1... | collective-permute-start | bytes 12296 | tf_op jit(solution)/shard_map/ppermute | solution.py:19
  255.0 8.3 %copy-start.10 = (bf16[128,128]{1,0:T(8,128)(2,1)S(1)}, bf16[128,128]{1,0:T(8,128)(2,1)}, u32[]{:S(2)}) copy-start(bf16[128,128]{1,0:T(8,128)(2,1)} %param.22) | copy-start | bytes 98308
  255.0 11.5 %copy-start.1 = (bf16[28,448,128]{2,1,0:T(8,128)(2,1)S(1)}, bf16[28,448,128]{2,1,0:T(8,128)(2,1)}, u32[]{:S(2)}) copy-start(bf16[28,448,128]{2,1,0:T(8,128)(2,1)} %get-tuple-element.559) | copy-start | bytes 9633796
  263.3 3.2 copy-start.20
  265.6 133.8 %copy-start.6 = (bf16[128,128]{1,0:T(8,128)(2,1)}, bf16[128,128]{1,0:T(8,128)(2,1)S(1)}, u32[]{:S(2)}) copy-start(bf16[128,128]{1,0:T(8,128)(2,1)S(1)} %fusion.87) | copy-start | bytes 98308
  266.6 1.4 copy-start.14
  266.6 3.2 copy-start.29
  269.8 1.9 copy-start.31
  271.7 34.7 %copy-start.17 = (f32[64,16]{0,1:T(8,128)S(1)}, f32[64,16]{0,1:T(8,128)}, u32[]{:S(2)}) copy-start(f32[64,16]{0,1:T(8,128)} %get-tuple-element.177) | copy-start | bytes 12292
  271.8 108.5 %copy-start.27 = (s32[128]{0:T(128)S(1)}, s32[128]{0:T(128)}, u32[]{:S(2)}) copy-start(s32[128]{0:T(128)} %param.28) | copy-start | bytes 1540
  271.8 109.3 %copy-start.24 = (s32[4,128,2]{1,2,0:T(2,128)S(1)}, s32[4,128,2]{1,2,0:T(2,128)}, u32[]{:S(2)}) copy-start(s32[4,128,2]{1,2,0:T(2,128)} %custom-call.2) | copy-start | bytes 12292
  306.4 83.7 %collective-permute-start.7 = (f32[64,16]{0,1:T(8,128)S(1)}, f32[64,16]{0,1:T(8,128)S(1)}, u32[]{:S(2)}, u32[]{:S(2)}) collective-permute-start(f32[64,16]{0,1:T(8,128)S(1)} %copy-done.17), channel_id=1, source_target_pairs={{1,0},{2,1},{3,2},{4,3},{5,4},{6,5},{7,6},{8,7},{9,8},{10,9},{11,1... | collective-permute-start | bytes 12296 | tf_op jit(solution)/shard_map/ppermute | solution.py:20
  378.4 19.5 %collective-permute-start.2 = (bf16[64,128]{1,0:T(8,128)(2,1)S(1)}, bf16[64,128]{1,0:T(8,128)(2,1)}, u32[]{:S(2)}, u32[]{:S(2)}) collective-permute-start(bf16[64,128]{1,0:T(8,128)(2,1)S(1)} %get-tuple-element.174), channel_id=1, source_target_pairs={{0,1},{1,2},{2,3},{3,4},{4,5},{5,6},{6,7},{7,8},{8,9},{9,10},{10,1... | collective-permute-start | bytes 49160 | tf_op jit(solution)/shard_map/ppermute | solution.py:19
  387.7 10.1 %collective-permute-start.3 = (bf16[64,128]{1,0:T(8,128)(2,1)S(1)}, bf16[64,128]{1,0:T(8,128)(2,1)}, u32[]{:S(2)}, u32[]{:S(2)}) collective-permute-start(bf16[64,128]{1,0:T(8,128)(2,1)S(1)} %get-tuple-element.175), channel_id=1, source_target_pairs={{1,0},{2,1},{3,2},{4,3},{5,4},{6,5},{7,6},{8,7},{9,8},{10,9},{11,1... | collective-permute-start | bytes 49160 | tf_op jit(solution)/shard_map/ppermute | solution.py:20
  444.5 1.3 copy-start.4
  445.8 2.0 copy-start.30
  445.8 3.1 copy-start.15
  445.8 3.1 copy-start.22
  445.8 3.7 copy-start.8
  445.8 3.7 copy-start.13
  445.8 3.7 copy-start.18
  446.9 0.9 copy-start.2
  446.9 3.5 copy-start.23
  450.3 1.7 copy-start.25
  451.6 3.7 copy-start.5
  451.6 3.7 copy-start.19
  452.0 3.7 copy-start.9
  452.0 4.9 copy-start.7
  452.0 4.9 copy-start.11
  452.1 4.9 copy-start.12
  453.1 4.5 copy-start.21
  458.1 7.2 %collective-permute-start.8 = (bf16[64,128]{1,0:T(8,128)(2,1)S(1)}, bf16[64,128]{1,0:T(8,128)(2,1)S(1)}, u32[]{:S(2)}, u32[]{:S(2)}) collective-permute-start(bf16[64,128]{1,0:T(8,128)(2,1)S(1)} %get-tuple-element.172), channel_id=1, source_target_pairs={{0,1},{1,2},{2,3},{3,4},{4,5},{5,6},{6,7},{7,8},{8,9},{9,10},{10,1... | collective-permute-start | bytes 49160 | tf_op jit(solution)/shard_map/ppermute | solution.py:19
  463.0 6.9 %collective-permute-start.9 = (bf16[64,128]{1,0:T(8,128)(2,1)S(1)}, bf16[64,128]{1,0:T(8,128)(2,1)S(1)}, u32[]{:S(2)}, u32[]{:S(2)}) collective-permute-start(bf16[64,128]{1,0:T(8,128)(2,1)S(1)} %get-tuple-element.173), channel_id=1, source_target_pairs={{1,0},{2,1},{3,2},{4,3},{5,4},{6,5},{7,6},{8,7},{9,8},{10,9},{11,1... | collective-permute-start | bytes 49160 | tf_op jit(solution)/shard_map/ppermute | solution.py:20
  484.3 4.6 collective-permute-start.10
  486.2 6.9 %collective-permute-start.11 = (bf16[64,128]{1,0:T(8,128)(2,1)S(1)}, bf16[64,128]{1,0:T(8,128)(2,1)S(1)}, u32[]{:S(2)}, u32[]{:S(2)}) collective-permute-start(bf16[64,128]{1,0:T(8,128)(2,1)S(1)} %get-tuple-element.171), channel_id=1, source_target_pairs={{1,0},{2,1},{3,2},{4,3},{5,4},{6,5},{7,6},{8,7},{9,8},{10,9},{11,1... | collective-permute-start | bytes 49160 | tf_op jit(solution)/shard_map/ppermute | solution.py:20
where the time goes:
time: 513 us; the launch traced here: 507 us
  matrix products  203 us (40%)
  starting transfers between devices  106 us (21%)
  local copies, waits for them, and re-layouts  91.5 us (18%)
  other arithmetic  68.3 us (13%)
  waiting for transfers between devices  35.5 us (7%)
    dot_general x112, matrix products, one_row(): jnp.dot(normed, tri_in[which], preferred_element_type=jnp.float32)  172 us
    ppermute x6, starting transfers between devices, with_halo(): after = lax.ppermute(leading, axis, down)  82.7 us
    gather x144, local copies, waits for them, and re-layouts  54.1 us
    reduce_sum x35, other arithmetic, normalize(): jnp.mean(centred * centred, -1, keepdims=True) + 1e-05  34.7 us
    reduce_sum x31, other arithmetic, normalize(): centred = values - jnp.mean(values, -1, keepdims=True)  29.8 us
    ppermute x6, waiting for transfers between devices, with_halo(): before = lax.ppermute(last, axis, up)  26.6 us
    ppermute x6, starting transfers between devices, with_halo(): before = lax.ppermute(last, axis, up)  23.4 us
    while x2, local copies, waits for them, and re-layouts, project_rows(): return lax.map(one_row, rows)  15.7 us
  transfers between devices with their start and end apart: 12, of which 3 were waited for; matrix products, arithmetic and copies ran while one was open for 14% of the time, Pallas kernels for 0%

commit v1 on v0

v1 whole, which is shorter than its diff:
```python
import functools

import jax
import jax.numpy as jnp
from jax import lax
from jax.experimental import pallas as pl
from jax.experimental.pallas import tpu as pltpu
from jax.sharding import PartitionSpec as P

QUERY_ATOMS = 32
KW = 128
HALO = 64
SLOT = 32
LANES = 128
VMEM_LIMIT = 56 * 1024 * 1024
MESH = pl.DeviceIdType.MESH
NT = (((1,), (1,)), ((), ()))
TN = (((0,), (0,)), ((), ()))


def with_halo(x, sides, width):
    for axis, dim in sides:
        peers, length = (lax.axis_size(axis), x.shape[dim])
        up = [(i, (i + 1) % peers) for i in range(peers - 1)]
        down = [(j, i) for i, j in up]
        last = lax.slice_in_dim(x, length - width, length, axis=dim)
        leading = lax.slice_in_dim(x, 0, width, axis=dim)
        before = lax.ppermute(last, axis, up)
        after = lax.ppermute(leading, axis, down)
        x = jnp.concatenate([before, x, after], axis=dim)
    return x


def sigmoid(x):
    return 0.5 * jnp.tanh(0.5 * x) + 0.5


def normalize(values, axis=-1):
    values = values.astype(jnp.float32)
    centred = values - jnp.mean(values, axis, keepdims=True)
    return centred * lax.rsqrt(jnp.mean(centred * centred, axis, keepdims=True) + 1e-05)


def dot(a, b, dims=None):
    if dims is None:
        return jnp.dot(a, b, preferred_element_type=jnp.float32)
    return lax.dot_general(a, b, dims, preferred_element_type=jnp.float32)


def project_kernel(rows, chunk, lane_tiles, x_ref, w_ref, a_ref, b_ref, a_acc, b_acc):
    step = pl.program_id(1)
    ch = w_ref.shape[0] // 4
    for r in range(rows):
        zn = normalize(x_ref[r]).astype(jnp.bfloat16)
        pad = lane_tiles * LANES - chunk
        if pad:
            zn = jnp.concatenate([zn, jnp.zeros((pad, zn.shape[1]), zn.dtype)], axis=0)
        parts = dot(w_ref[...], zn, NT)
        left = sigmoid(parts[0:ch]) * parts[ch : 2 * ch]
        right = sigmoid(parts[2 * ch : 3 * ch]) * parts[3 * ch : 4 * ch]
        row = step * rows + r
        for q in range(lane_tiles):
            cols = slice(q * LANES, (q + 1) * LANES)
            a_acc[q, pl.ds(row, ch, stride=SLOT), :] = left[:, cols]
            b_acc[q, pl.ds(row, ch, stride=SLOT), :] = right[:, cols]

    @pl.when(step == pl.num_programs(1) - 1)
    def _():
        a_ref[0] = a_acc[...].astype(jnp.bfloat16)
        b_ref[0] = b_acc[...].astype(jnp.bfloat16)


def project(x, w, chunk):
    tok_dev, span, width = x.shape
    ch = w.shape[0] // 4
    rows = 4
    tiles = -(-chunk // LANES)
    shape = (tiles, ch * SLOT, LANES)
    out = jax.ShapeDtypeStruct((span // chunk,) + shape, jnp.bfloat16)
    out_spec = pl.BlockSpec((1,) + shape, lambda k, i: (k, 0, 0, 0))
    return pl.pallas_call(
        functools.partial(project_kernel, rows, chunk, tiles),
        grid=(span // chunk, tok_dev // rows),
        in_specs=[
            pl.BlockSpec((rows, chunk, width), lambda k, i: (i, k, 0)),
            pl.BlockSpec(w.shape, lambda k, i: (0, 0)),
        ],
        out_specs=[out_spec, out_spec],
        out_shape=[out, out],
        scratch_shapes=[pltpu.VMEM(shape, jnp.float32)] * 2,
        compiler_params=pltpu.CompilerParams(vmem_limit_bytes=VMEM_LIMIT),
        cost_estimate=pl.CostEstimate(
            flops=2 * x.size * 4 * ch, bytes_accessed=6 * x.size, transcendentals=2 * x.size
        ),
        name="project",
    )(x, w)


def product_kernel(ch, ao_ref, bo_ref, an_ref, bn_ref, out_ref):
    quarter = ch // 4
    half = ch // 2
    tiles = ao_ref.shape[1]

    @pl.when(pl.program_id(0) == 0)
    def _():
        out_ref[...] = jnp.zeros_like(out_ref)

    def load(ref, at):
        return jnp.concatenate([ref[0, q, pl.ds(at, SLOT), :] for q in range(tiles)], axis=1)

    def group(g, carry):
        outs = []
        for cl in range(4):
            at = pl.multiple_of((cl * quarter + g) * SLOT, SLOT)
            left = jnp.concatenate([load(ao_ref, at), load(an_ref, at)], axis=0)
            right = jnp.concatenate([load(bo_ref, at), load(bn_ref, at)], axis=0)
            outs.append(dot(left, right, NT))
        first = pl.ds(pl.multiple_of(g * SLOT, SLOT), SLOT)
        second = pl.ds(pl.multiple_of((quarter + g) * SLOT, SLOT), SLOT)
        third = pl.ds(pl.multiple_of((half + g) * SLOT, SLOT), SLOT)
        out_ref[first, :] += jnp.concatenate([outs[0][:SLOT], outs[2][:SLOT]], axis=1)
        out_ref[second, :] += jnp.concatenate([outs[1][:SLOT], outs[3][:SLOT]], axis=1)
        out_ref[third, :] += jnp.concatenate([o[SLOT:, :SLOT] for o in outs], axis=1)
        return carry

    lax.fori_loop(0, quarter, group, 0)


def product(own, low, ch):
    chunks, tiles, rows, lanes = own[0].shape
    spec = pl.BlockSpec((1, tiles, rows, lanes), lambda k: (k, 0, 0, 0))
    out_rows = (ch // 2 + ch // 4) * SLOT
    return pl.pallas_call(
        functools.partial(product_kernel, ch),
        grid=(chunks,),
        in_specs=[spec] * 4,
        out_specs=pl.BlockSpec((out_rows, LANES), lambda k: (0, 0)),
        out_shape=jax.ShapeDtypeStruct((out_rows, LANES), jnp.float32),
        compiler_params=pltpu.CompilerParams(vmem_limit_bytes=VMEM_LIMIT),
        name="product",
    )(own[0], own[1], low[0], low[1])


def tail_kernel(rows, tok_dev, ch, p1_ref, p2_ref, d_ref, band_ref, gate_ref, out_w_ref,
                proj_ref, band_out_ref, table_ref):
    step = pl.program_id(0)
    half, quarter = ch // 2, ch // 4
    cp = proj_ref.shape[0]

    @pl.when(step == 0)
    def _():
        table_ref[...] = jnp.zeros_like(table_ref)

    for r in range(rows):
        row = step * rows + r
        near = pl.ds(row, half, stride=SLOT)
        main = p1_ref[near, :] + p2_ref[near, :]
        main = jnp.concatenate([main[:, :64], main[:, 64:]], axis=0)
        above = d_ref[pl.ds(row, quarter, stride=SLOT), :]
        above = jnp.concatenate([above[:, q * SLOT : (q + 1) * SLOT] for q in range(4)], axis=0)
        prod = jnp.concatenate([main, above, above], axis=1)
        pn = normalize(prod, 0).astype(jnp.bfloat16)
        update = dot(pn, out_w_ref[...], TN)
        update = jnp.concatenate(
            [update[SLOT : SLOT + tok_dev], update[:tok_dev], update[64 : 64 + tok_dev]], axis=0
        )
        band = band_ref[r].astype(jnp.float32)
        gate = sigmoid(dot(normalize(band).astype(jnp.bfloat16), gate_ref[...]))
        new = (band + gate * update).astype(jnp.bfloat16)
        band_out_ref[r] = new
        zt = normalize(new)
        zt = jnp.concatenate([zt, jnp.zeros((LANES - 3 * tok_dev, zt.shape[1]), zt.dtype)], axis=0)
        tok = dot(proj_ref[...], zt.astype(jnp.bfloat16), NT)
        table_ref[pl.ds(row, cp, stride=SLOT), :] = tok


def tail(p1, p2, d, band, tri_gate, tri_out, proj_t):
    tok_dev, width, c = band.shape
    ch = tri_out.shape[0]
    cp = proj_t.shape[0]
    rows = 4
    whole = lambda x: pl.BlockSpec(x.shape, lambda i: (0, 0))
    band_spec = pl.BlockSpec((rows, width, c), lambda i: (i, 0, 0))
    return pl.pallas_call(
        functools.partial(tail_kernel, rows, tok_dev, ch),
        grid=(tok_dev // rows,),
        in_specs=[whole(p1), whole(p2), whole(d), band_spec, whole(tri_gate), whole(tri_out),
                  whole(proj_t)],
        out_specs=[band_spec, pl.BlockSpec((cp * SLOT, LANES), lambda i: (0, 0))],
        out_shape=[
            jax.ShapeDtypeStruct(band.shape, jnp.bfloat16),
            jax.ShapeDtypeStruct((cp * SLOT, LANES), jnp.float32),
        ],
        compiler_params=pltpu.CompilerParams(vmem_limit_bytes=VMEM_LIMIT),
        name="tail",
    )(p1, p2, d, band, tri_gate, tri_out, proj_t)


def atom_kernel(devices, heads, blocks, mix_ref, table_ref, qtok_ref, ktok_ref, valid_ref,
                offset_ref, cq_ref, ck_ref, act_ref, cond_ref, w_ref, out_ref,
                ext, bias, planes, send_sem, recv_sem):
    atoms, width = act_ref.shape
    span = atoms + 2 * HALO
    cp = ck_ref.shape[0]
    head_dim = width // heads
    me = lax.axis_index("tok") * 2 + lax.axis_index("atm")
    above, below = me + 1, me - 1
    has_above, has_below = me < devices - 1, me > 0

    def place(d):
        d = jnp.clip(d, 0, devices - 1)
        return (d // 2, d % 2)

    barrier = pltpu.get_barrier_semaphore()

    @pl.when(has_below)
    def _():
        pl.semaphore_signal(barrier, inc=1, device_id=place(below), device_id_type=MESH)

    @pl.when(has_above)
    def _():
        pl.semaphore_signal(barrier, inc=1, device_id=place(above), device_id_type=MESH)

    def copies(b):
        up = pltpu.make_async_remote_copy(
            src_ref=ext.at[b, pl.ds(atoms, HALO)],
            dst_ref=ext.at[b, pl.ds(0, HALO)],
            send_sem=send_sem.at[b, 0],
            recv_sem=recv_sem.at[b, 0],
            device_id=place(above),
            device_id_type=MESH,
        )
        down = pltpu.make_async_remote_copy(
            src_ref=ext.at[b, pl.ds(HALO, HALO)],
            dst_ref=ext.at[b, pl.ds(HALO + atoms, HALO)],
            send_sem=send_sem.at[b, 1],
            recv_sem=recv_sem.at[b, 1],
            device_id=place(below),
            device_id_type=MESH,
        )
        return up, down

    @pl.when(jnp.logical_not(has_below))
    def _():
        for b in range(blocks):
            ext[b, pl.ds(0, HALO)] = jnp.zeros((HALO, width), jnp.bfloat16)

    @pl.when(jnp.logical_not(has_above))
    def _():
        for b in range(blocks):
            ext[b, pl.ds(HALO + atoms, HALO)] = jnp.zeros((HALO, width), jnp.bfloat16)

    cond = normalize(cond_ref[...]).astype(jnp.bfloat16)
    state = act_ref[...].astype(jnp.float32)
    scales = [sigmoid(dot(cond, w_ref[b, 0])) for b in range(blocks)]
    shifts = [dot(cond, w_ref[b, 1]) for b in range(blocks)]

    def begin(b, state):
        normed = (scales[b] * normalize(state) + shifts[b]).astype(jnp.bfloat16)
        ext[b, pl.ds(HALO, atoms)] = normed
        if b == 0:

            @pl.when(jnp.logical_and(has_below, has_above))
            def _():
                pl.semaphore_wait(barrier, 2)

            @pl.when(jnp.logical_not(jnp.logical_and(has_below, has_above)))
            def _():
                pl.semaphore_wait(barrier, 1)

        up, down = copies(b)

        @pl.when(has_above)
        def _():
            up.start()

        @pl.when(has_below)
        def _():
            down.start()

        return normed

    def finish(b):
        up, down = copies(b)

        @pl.when(has_above)
        def _():
            up.wait_send()
            down.wait_recv()

        @pl.when(has_below)
        def _():
            down.wait_send()
            up.wait_recv()

    normed = begin(0, state)

    qhot = (qtok_ref[...] == lax.broadcasted_iota(jnp.int32, (atoms, SLOT), 1)).astype(jnp.float32)
    qhot = qhot.astype(jnp.bfloat16)
    khot = (ktok_ref[...] == lax.broadcasted_iota(jnp.int32, (LANES, span), 0)).astype(jnp.float32)
    khot = khot.astype(jnp.bfloat16)
    picked = dot(table_ref[...].astype(jnp.bfloat16), khot).astype(jnp.bfloat16)
    for c in range(cp):
        sel = dot(qhot, picked[c * SLOT : (c + 1) * SLOT])
        planes[c] = sel + cq_ref[:, c : c + 1] + ck_ref[c : c + 1, :]
    key = lax.broadcasted_iota(jnp.int32, (atoms, span), 1)
    begin_key = offset_ref[...]
    live = jnp.logical_and(key >= begin_key, key < begin_key + KW)
    live = jnp.logical_and(live, valid_ref[...] > 0)
    outs = blocks * heads
    rows = 16

    def mix(g, carry):
        at = pl.ds(pl.multiple_of(g * rows, rows), rows)
        total = [None] * outs
        for c in range(cp):
            base = planes[c, at, :]
            positive = jnp.maximum(base, 0.0)
            for o in range(outs):
                term = base * mix_ref[c, o] + positive * mix_ref[cp + c, o]
                total[o] = term if c == 0 else total[o] + term
        for o in range(outs):
            bias[o, at, :] = total[o]
        return carry

    lax.fori_loop(0, atoms // rows, mix, 0)

    for b in range(blocks):
        if b:
            normed = begin(b, state)
        queries = (dot(normed, w_ref[b, 2]) * head_dim**-0.5).astype(jnp.bfloat16)
        gates = sigmoid(dot(normed, w_ref[b, 5]))
        finish(b)
        full = ext[b]
        keys = dot(full, w_ref[b, 3]).astype(jnp.bfloat16)
        values = dot(full, w_ref[b, 4]).astype(jnp.bfloat16)
        blended = []
        for h in range(heads):
            cols = slice(h * head_dim, (h + 1) * head_dim)
            logits = dot(queries[:, cols], keys[:, cols], NT) + bias[b * heads + h]
            logits = jnp.where(live, logits, -1e30)
            weights = jnp.exp(logits - jnp.max(logits, -1, keepdims=True))
            probs = (weights / jnp.sum(weights, -1, keepdims=True)).astype(jnp.bfloat16)
            blended.append(dot(probs, values[:, cols]))
        attended = (jnp.concatenate(blended, axis=1) * gates).astype(jnp.bfloat16)
        state = state + dot(attended, w_ref[b, 6])
    out_ref[...] = state.astype(jnp.bfloat16)


def atoms_part(mix, table, qtok, ktok, valid, offset, cq, ck, act, cond, weights, devices, heads):
    atoms, width = act.shape
    span = atoms + 2 * HALO
    blocks = weights.shape[0]
    vmem = pl.BlockSpec(memory_space=pltpu.VMEM)
    return pl.pallas_call(
        functools.partial(atom_kernel, devices, heads, blocks),
        in_specs=[pl.BlockSpec(memory_space=pltpu.SMEM)] + [vmem] * 10,
        out_specs=vmem,
        out_shape=jax.ShapeDtypeStruct(act.shape, jnp.bfloat16),
        scratch_shapes=[
            pltpu.VMEM((blocks, span, width), jnp.bfloat16),
            pltpu.VMEM((blocks * heads, atoms, span), jnp.float32),
            pltpu.VMEM((ck.shape[0], atoms, span), jnp.float32),
            pltpu.SemaphoreType.DMA((blocks, 2)),
            pltpu.SemaphoreType.DMA((blocks, 2)),
        ],
        compiler_params=pltpu.CompilerParams(
            collective_id=0, has_side_effects=True, vmem_limit_bytes=VMEM_LIMIT
        ),
        name="atoms",
    )(mix, table, qtok, ktok, valid, offset, cq, ck, act, cond, weights)


def local(
    pair,
    tri_in,
    tri_gate,
    tri_out,
    pair_proj,
    atom_act,
    atom_cond,
    cond_pair,
    pair_mlp,
    bias_proj,
    block_weights,
    atom_token,
    atom_mask,
    key_start,
    key_tiles,
):
    tok_dev, tokens, _ = pair.shape
    groups = lax.axis_size("tok")
    ch = tri_in.shape[2]
    shard = lax.axis_index("tok")
    core = lax.axis_index("atm")
    up = [(i, i + 1) for i in range(groups - 1)]
    down = [(i + 1, i) for i in range(groups - 1)]

    half = tokens // 2
    chunk = 8 * tok_dev
    own = lax.dynamic_slice_in_dim(pair, core * half, half, 1)
    low = lax.ppermute(own, "tok", up)
    w = jnp.swapaxes(tri_in, 1, 2).reshape(4 * ch, -1)
    partial = product(project(own, w, chunk), project(low, w, chunk), ch)
    other = lax.ppermute(partial, "atm", [(0, 1), (1, 0)])
    main_rows = ch // 2 * SLOT
    back = (partial[main_rows:] + other[main_rows:]).astype(jnp.bfloat16)
    back = lax.ppermute(back, "tok", down).astype(jnp.float32)

    padded = jnp.pad(pair, ((0, 0), (tok_dev, tok_dev), (0, 0)))
    band = lax.dynamic_slice_in_dim(padded, shard * tok_dev, 3 * tok_dev, 1)
    pair_band, table = tail(partial, other, back, band, tri_gate, tri_out, pair_proj.T)

    atoms = atom_act.shape[0]
    heads = bias_proj.shape[2]
    device = shard * lax.axis_size("atm") + core
    labels = jnp.stack([atom_token, atom_mask], 1)
    labels_ext = with_halo(labels, ((("tok", "atm"), 0),), HALO)
    relu_cond = jax.nn.relu(atom_cond)
    query_term = jnp.dot(relu_cond, cond_pair[0], preferred_element_type=jnp.float32)
    key_term = jnp.dot(relu_cond, cond_pair[1], preferred_element_type=jnp.float32)
    key_term_ext = with_halo(key_term, ((("tok", "atm"), 0),), HALO)
    offsets = key_start - device * atoms + HALO
    projections = jnp.swapaxes(bias_proj, 0, 1).reshape(bias_proj.shape[1], -1).astype(jnp.float32)
    mixed = jnp.dot(
        pair_mlp.astype(jnp.float32), projections, precision=lax.Precision.HIGHEST
    )
    atoms_out = atoms_part(
        jnp.concatenate([projections, mixed], 0),
        table,
        (atom_token - shard * tok_dev)[:, None],
        (labels_ext[:, 0] - (shard - 1) * tok_dev)[None, :],
        labels_ext[:, 1][None, :],
        jnp.repeat(offsets, QUERY_ATOMS)[:, None],
        query_term,
        key_term_ext.T,
        atom_act,
        atom_cond,
        block_weights,
        groups * lax.axis_size("atm"),
        heads,
    )
    return (pair_band, atoms_out)


def solution(mesh):
    in_specs = (
        P("tok", None, None),
        P(),
        P(),
        P(),
        P(),
        P(("tok", "atm"), None),
        P(("tok", "atm"), None),
        P(),
        P(),
        P(),
        P(),
        P(("tok", "atm")),
        P(("tok", "atm")),
        P(("tok", "atm")),
        P(("tok", "atm"), None),
    )
    out_specs = (P("tok", None, None), P(("tok", "atm"), None))
    return jax.shard_map(local, mesh=mesh, in_specs=in_specs, out_specs=out_specs, check_vma=False)
```

time: 513 us -> 129 us (0.25)
  matrix products: 203 us -> 0.99 us
  starting transfers between devices: 106 us -> 19.2 us
  local copies, waits for them, and re-layouts: 91.5 us -> 6.63 us
  Pallas kernels: 0 us -> 74.2 us
  other arithmetic: 68.3 us -> 4.09 us
  waiting for transfers between devices: 35.5 us -> 21.9 us
    dot_general x146 -> x1, matrix products: 202 us -> 0.12 us  [local(): jnp.dot(pair_mlp.astype(jnp.float32), projections, precision=lax.Precisio...]
    ppermute x6 -> x2, starting transfers between devices: 82.7 us -> 3.84 us  [with_halo(): after = lax.ppermute(leading, axis, down)]
    pallas_call x0 -> x5, Pallas kernels: none -> 74.2 us  [the longest x2 29 us: project(): pl.pallas_call(functools.partial(project_kernel, rows, chunk, tiles), gri...]
    reduce_sum x66 -> x0, other arithmetic: 64.5 us -> none  [the longest x35 34.7 us: normalize(): jnp.mean(centred * centred, -1, keepdims=True) + 1e-05]
    gather x144 -> x0, local copies, waits for them, and re-layouts: 54.1 us -> none
    ppermute x6 -> x2, waiting for transfers between devices: 26.6 us -> 0.01 us  [with_halo(): before = lax.ppermute(last, axis, up)]
    ppermute x0 -> x3, waiting for transfers between devices: none -> 21.9 us  [the longest x1 13.6 us: local(): low = lax.ppermute(own, 'tok', up)]
    while x2 -> x0, local copies, waits for them, and re-layouts: 15.7 us -> none  [project_rows(): return lax.map(one_row, rows)]
  transfers between devices with their start and end apart: 12 -> 7, of which waited for: 3 -> 2; matrix products, arithmetic and copies ran while one was open for 14% -> 6% of each run, Pallas kernels for 0% -> 33%
where the time goes in v1:
time: 129 us; the launch traced here: 128 us
  Pallas kernels  74.2 us (58%)
  waiting for transfers between devices  21.9 us (17%)
  starting transfers between devices  19.2 us (15%)
  local copies, waits for them, and re-layouts  6.63 us (5%)
  other arithmetic  4.09 us (3%)
    pallas_call x2, Pallas kernels, project(): pl.pallas_call(functools.partial(project_kernel, rows, chunk, tiles), gri...  29 us
    pallas_call x1, Pallas kernels, atoms_part(): pl.pallas_call(functools.partial(atom_kernel, devices, heads, blocks), in...  18 us
    pallas_call x1, Pallas kernels, tail(): pl.pallas_call(functools.partial(tail_kernel, rows, tok_dev, ch), grid=(t...  14.5 us
    ppermute x1, waiting for transfers between devices, local(): low = lax.ppermute(own, 'tok', up)  13.6 us
    pallas_call x1, Pallas kernels, product(): pl.pallas_call(functools.partial(product_kernel, ch), grid=(chunks,), in_...  12.7 us
    ppermute x2, starting transfers between devices, with_halo(): before = lax.ppermute(last, axis, up)  8.79 us
    ppermute x1, waiting for transfers between devices, local(): back = lax.ppermute(back, 'tok', down).astype(jnp.float32)  8.29 us
    ppermute x2, starting transfers between devices, with_halo(): after = lax.ppermute(leading, axis, down)  3.84 us
  transfers between devices with their start and end apart: 7, of which 2 were waited for; matrix products, arithmetic and copies ran while one was open for 6% of the time, Pallas kernels for 33%

profile of v1, /device:TPU:23, one launch (start us, length us, event | category | flops | bytes accessed | tf_op | source)
XLA Modules:
  0.0 127.9 jit_solution(8449285966407694905)
XLA Ops:
  0.6 0.0 copy-start
  0.6 0.0 copy-start.7
  0.7 1.6 %constant_dynamic-slice_fusion.x_ref = bf16[28,224,128]{2,1,0:T(8,128)(2,1)S(1)} fusion(bf16[28,448,128]{2,1,0:T(8,128)(2,1)} %param.15, s32[]{:T(128)S(6)} %select_n.6), kind=kLoop, calls=%fused_computation.22 | loop fusion | bytes 3211268 | tf_op jit(solution)/shard_map/dynamic_slice | solution.py:401
  2.3 0.0 copy-start.2
  2.3 3.1 %collective-permute-start = (bf16[28,224,128]{2,1,0:T(8,128)(2,1)S(1)}, bf16[28,224,128]{2,1,0:T(8,128)(2,1)}, u32[]{:S(2)}, u32[]{:S(2)}) collective-permute-start(bf16[28,224,128]{2,1,0:T(8,128)(2,1)S(1)} %constant_dynamic-slice_fusion.x_ref), channel_id=1, source_target_pairs={{0,2},{2,4},{4,6},{6,8},{8,10},{10,12},{12,14},{14,16},{16,18},{18... | collective-permute-start | bytes 4816904 | tf_op jit(solution)/shard_map/ppermute | solution.py:402
  5.4 0.0 copy-done.7
  5.4 0.0 copy-done.8
  5.4 0.1 fusion.15
  5.5 3.9 %collective-permute-start.3 = (s32[64,2]{0,1:T(2,128)S(1)}, s32[64,2]{0,1:T(2,128)S(1)}, u32[]{:S(2)}, u32[]{:S(2)}) collective-permute-start(s32[64,2]{0,1:T(2,128)S(1)} %get-tuple-element.18), channel_id=1, source_target_pairs={{0,1},{1,2},{2,3},{3,4},{4,5},{5,6},{6,7},{7,8},{8,9},{9,10},{10,1... | collective-permute-start | bytes 1544 | tf_op jit(solution)/shard_map/ppermute | solution.py:28
  9.5 1.9 %collective-permute-start.4 = (s32[64,2]{0,1:T(2,128)S(1)}, s32[64,2]{0,1:T(2,128)S(1)}, u32[]{:S(2)}, u32[]{:S(2)}) collective-permute-start(s32[64,2]{0,1:T(2,128)S(1)} %get-tuple-element.19), channel_id=1, source_target_pairs={{1,0},{2,1},{3,2},{4,3},{5,4},{6,5},{7,6},{8,7},{9,8},{10,9},{11,1... | collective-permute-start | bytes 1544 | tf_op jit(solution)/shard_map/ppermute | solution.py:29
  11.4 0.8 copy.22
  12.2 0.0 copy-done.2
  12.2 14.5 %project.2 = (bf16[1,2,4096,128]{3,2,1,0:T(8,128)(2,1)}, bf16[1,2,4096,128]{3,2,1,0:T(8,128)(2,1)}) custom-call(bf16[28,224,128]{2,1,0:T(8,128)(2,1)} %copy-done.2, bf16[512,128]{1,0:T(8,128)(2,1)} %bitcast.25), custom_call_target="tpu_custom_call" | custom-call | flops 822083584 | bytes 4816896 | tf_op jit(solution)/shard_map/project/pallas_call | solution.py:81
  26.7 13.6 %collective-permute-done.x_ref = bf16[28,224,128]{2,1,0:T(8,128)(2,1)} collective-permute-done((bf16[28,224,128]{2,1,0:T(8,128)(2,1)S(1)}, bf16[28,224,128]{2,1,0:T(8,128)(2,1)}, u32[]{:S(2)}, u32[]{:S(2)}) %collective-permute-start) | collective-permute-done | bytes 1605664 | tf_op jit(solution)/shard_map/ppermute | solution.py:402
  40.2 14.5 %project.3 = (bf16[1,2,4096,128]{3,2,1,0:T(8,128)(2,1)}, bf16[1,2,4096,128]{3,2,1,0:T(8,128)(2,1)}) custom-call(bf16[28,224,128]{2,1,0:T(8,128)(2,1)} %collective-permute-done.x_ref, bf16[512,128]{1,0:T(8,128)(2,1)} %bitcast.26), custom_call_target="tpu_custom_call" | custom-call | flops 822083584 | bytes 4816896 | tf_op jit(solution)/shard_map/project/pallas_call | solution.py:81
  54.8 0.0 copy-start.1
  54.8 12.7 %product.1.p1_ref = f32[3072,128]{1,0:T(8,128)} custom-call(bf16[1,2,4096,128]{3,2,1,0:T(8,128)(2,1)} %get-tuple-element.8.ao_ref, bf16[1,2,4096,128]{3,2,1,0:T(8,128)(2,1)} %get-tuple-element.9.bo_ref, bf16[1,2,4096,128]{3,2,1,0:T(8,128)(2,1)} %get-tuple-element.10.an_ref, bf16[1,2,4096,128]{3,2,1,0:T(8,128)(2,1)} %get-tuple-element.11.bn_ref), custom_call_target="tpu_custom_call" | custom-call | tf_op jit(solution)/shard_map/product/pallas_call | solution.py:133
  67.5 1.6 %collective-permute-start.1 = (f32[3072,128]{1,0:T(8,128)}, f32[3072,128]{1,0:T(8,128)}, u32[]{:S(2)}, u32[]{:S(2)}) collective-permute-start(f32[3072,128]{1,0:T(8,128)} %product.1.p1_ref), channel_id=1, source_target_pairs={{0,1},{1,0},{2,3},{3,2},{4,5},{5,4},{6,7},{7,6},{8,9},{9,8},{10,11... | collective-permute-start | bytes 4718600 | tf_op jit(solution)/shard_map/ppermute | solution.py:405
  69.1 0.0 copy-done.5
  69.1 0.1 fusion.1
  69.2 0.1 fusion.14
  69.3 4.8 %collective-permute-start.5 = (f32[64,16]{0,1:T(8,128)S(1)}, f32[64,16]{0,1:T(8,128)S(1)}, u32[]{:S(2)}, u32[]{:S(2)}) collective-permute-start(f32[64,16]{0,1:T(8,128)S(1)} %get-tuple-element.14), channel_id=1, source_target_pairs={{0,1},{1,2},{2,3},{3,4},{4,5},{5,6},{6,7},{7,8},{8,9},{9,10},{10,1... | collective-permute-start | bytes 12296 | tf_op jit(solution)/shard_map/ppermute | solution.py:28
  74.1 1.9 %collective-permute-start.6 = (f32[64,16]{0,1:T(8,128)S(1)}, f32[64,16]{0,1:T(8,128)S(1)}, u32[]{:S(2)}, u32[]{:S(2)}) collective-permute-start(f32[64,16]{0,1:T(8,128)S(1)} %get-tuple-element.15), channel_id=1, source_target_pairs={{1,0},{2,1},{3,2},{4,3},{5,4},{6,5},{7,6},{8,7},{9,8},{10,9},{11,1... | collective-permute-start | bytes 12296 | tf_op jit(solution)/shard_map/ppermute | solution.py:29
  76.1 0.0 copy-done.6
  76.1 0.1 copy.23
  76.2 1.1 pad_dynamic-slice_fusion.band_ref
  77.3 0.0 copy-done.9
  77.3 0.1 fusion.16
  77.4 0.7 fusion.3.cq_ref
  78.2 0.6 pad_maximum_fusion.mix_ref
  78.8 0.7 copy.25.qtok_ref
  79.5 0.1 broadcast_in_dim.8
  79.6 0.7 broadcast_in_dim_reshape.4.offset_ref
  80.3 0.0 collective-permute-done.3
  80.3 0.0 collective-permute-done.4
  80.3 0.1 pad_add_fusion
  80.4 0.0 collective-permute-done.1.p2_ref
  80.4 1.3 fusion
  81.7 1.9 %collective-permute-start.2 = (bf16[1024,128]{1,0:T(8,128)(2,1)S(1)}, bf16[1024,128]{1,0:T(8,128)(2,1)S(1)}, u32[]{:S(2)}, u32[]{:S(2)}) collective-permute-start(bf16[1024,128]{1,0:T(8,128)(2,1)S(1)} %fusion), channel_id=1, source_target_pairs={{2,0},{4,2},{6,4},{8,6},{10,8},{12,10},{14,12},{16,14},{18,16},{20... | collective-permute-start | bytes 786440 | tf_op jit(solution)/shard_map/ppermute | solution.py:408
  83.6 0.6 slice_bitcast_fusion
  84.2 0.0 collective-permute-done.5
  84.2 0.0 collective-permute-done.6
  84.2 0.7 maximum_bitcast_fusion.ck_ref
  84.9 8.3 %collective-permute-done.2 = bf16[1024,128]{1,0:T(8,128)(2,1)S(1)} collective-permute-done((bf16[1024,128]{1,0:T(8,128)(2,1)S(1)}, bf16[1024,128]{1,0:T(8,128)(2,1)S(1)}, u32[]{:S(2)}, u32[]{:S(2)}) %collective-permute-start.2) | collective-permute-done | bytes 262176 | tf_op jit(solution)/shard_map/ppermute | solution.py:408
  93.2 0.8 convert_element_type.13.d_ref
  94.0 14.5 %tail.1 = (bf16[28,84,128]{2,1,0:T(8,128)(2,1)}, f32[512,128]{1,0:T(8,128)}) custom-call(f32[3072,128]{1,0:T(8,128)} %product.1.p1_ref, f32[3072,128]{1,0:T(8,128)} %collective-permute-done.1.p2_ref, f32[1024,128]{1,0:T(8,128)} %convert_element_type.13.d_ref, bf16[28,84,128]{2,1,0:T(8,128)(2,1)} %pad_dynamic-slice_fusion.band_ref, ...), custom_call_target="tpu_custom_call" | custom-call | tf_op jit(solution)/shard_map/tail/pallas_call | solution.py:184
  108.5 18.0 %atoms.1 = bf16[128,128]{1,0:T(8,128)(2,1)} custom-call(f32[32,12]{1,0:T(8,128)} %pad_maximum_fusion.mix_ref, f32[512,128]{1,0:T(8,128)} %get-tuple-element.13.table_ref, s32[128,1]{1,0:T(8,128)} %copy.25.qtok_ref, s32[1,256]{1,0:T(1,128)} %get-tuple-element.17.ktok_ref, s32[1,256]{1,0:T(1,128)} %get-tuple-element.16.valid_ref, ...), custom_call_target="tpu_custom_call" | custom-call | tf_op jit(solution)/shard_map/atoms/pallas_call | solution.py:355
  126.5 1.4 %copy.31 = bf16[128,128]{1,0:T(8,128)(2,1)} copy(bf16[128,128]{1,0:T(8,128)(2,1)} %atoms.1) | data formatting | bytes 65536
  (15 shorter events, 0.1 us)
Async XLA Ops:
  0.6 76.7 %copy-start = (bf16[16,16]{1,0:T(8,128)(2,1)S(1)}, bf16[16,16]{1,0:T(8,128)(2,1)}, u32[]{:S(2)}) copy-start(bf16[16,16]{1,0:T(8,128)(2,1)} %param.23) | copy-start | bytes 1540
  0.6 4.8 %copy-start.7 = (s32[128]{0:T(128)S(1)}, s32[128]{0:T(128)}, u32[]{:S(2)}) copy-start(s32[128]{0:T(128)} %param.26) | copy-start | bytes 1540
  0.7 4.8 %copy-start.8 = (s32[128]{0:T(128)S(1)}, s32[128]{0:T(128)}, u32[]{:S(2)}) copy-start(s32[128]{0:T(128)} %param.27) | copy-start | bytes 1540
  0.7 10.7 %copy-start.4 = (bf16[4,128,128]{2,1,0:T(8,128)(2,1)S(1)}, bf16[4,128,128]{2,1,0:T(8,128)(2,1)}, u32[]{:S(2)}) copy-start(bf16[4,128,128]{2,1,0:T(8,128)(2,1)} %param.16) | copy-start | bytes 393220
  2.3 9.9 %copy-start.2 = (bf16[28,224,128]{2,1,0:T(8,128)(2,1)}, bf16[28,224,128]{2,1,0:T(8,128)(2,1)S(1)}, u32[]{:S(2)}) copy-start(bf16[28,224,128]{2,1,0:T(8,128)(2,1)S(1)} %constant_dynamic-slice_fusion.x_ref) | copy-start | bytes 4816900
  2.3 38.0 %collective-permute-start = (bf16[28,224,128]{2,1,0:T(8,128)(2,1)S(1)}, bf16[28,224,128]{2,1,0:T(8,128)(2,1)}, u32[]{:S(2)}, u32[]{:S(2)}) collective-permute-start(bf16[28,224,128]{2,1,0:T(8,128)(2,1)S(1)} %constant_dynamic-slice_fusion.x_ref), channel_id=1, source_target_pairs={{0,2},{2,4},{4,6},{6,8},{8,10},{10,12},{12,14},{14,16},{16,18},{18... | collective-permute-start | bytes 4816904 | tf_op jit(solution)/shard_map/ppermute | solution.py:402
  5.5 74.8 %collective-permute-start.3 = (s32[64,2]{0,1:T(2,128)S(1)}, s32[64,2]{0,1:T(2,128)S(1)}, u32[]{:S(2)}, u32[]{:S(2)}) collective-permute-start(s32[64,2]{0,1:T(2,128)S(1)} %get-tuple-element.18), channel_id=1, source_target_pairs={{0,1},{1,2},{2,3},{3,4},{4,5},{5,6},{6,7},{7,8},{8,9},{9,10},{10,1... | collective-permute-start | bytes 1544 | tf_op jit(solution)/shard_map/ppermute | solution.py:28
  9.5 70.8 %collective-permute-start.4 = (s32[64,2]{0,1:T(2,128)S(1)}, s32[64,2]{0,1:T(2,128)S(1)}, u32[]{:S(2)}, u32[]{:S(2)}) collective-permute-start(s32[64,2]{0,1:T(2,128)S(1)} %get-tuple-element.19), channel_id=1, source_target_pairs={{1,0},{2,1},{3,2},{4,3},{5,4},{6,5},{7,6},{8,7},{9,8},{10,9},{11,1... | collective-permute-start | bytes 1544 | tf_op jit(solution)/shard_map/ppermute | solution.py:29
  54.8 14.3 %copy-start.3 = (bf16[128,128]{1,0:T(8,128)(2,1)S(1)}, bf16[128,128]{1,0:T(8,128)(2,1)}, u32[]{:S(2)}) copy-start(bf16[128,128]{1,0:T(8,128)(2,1)} %cond_ref.1) | copy-start | bytes 98308
  54.8 14.3 %copy-start.5 = (bf16[2,128,16]{1,2,0:T(8,128)(2,1)S(1)}, bf16[2,128,16]{1,2,0:T(8,128)(2,1)}, u32[]{:S(2)}) copy-start(bf16[2,128,16]{1,2,0:T(8,128)(2,1)} %param.22) | copy-start | bytes 24580
  54.8 21.3 %copy-start.6 = (bf16[3,16,4]{1,2,0:T(4,128)(2,1)S(1)}, bf16[3,16,4]{1,2,0:T(4,128)(2,1)}, u32[]{:S(2)}) copy-start(bf16[3,16,4]{1,2,0:T(4,128)(2,1)} %param.24) | copy-start | bytes 1156
  54.8 21.4 %copy-start.1 = (bf16[28,448,128]{2,1,0:T(8,128)(2,1)S(1)}, bf16[28,448,128]{2,1,0:T(8,128)(2,1)}, u32[]{:S(2)}) copy-start(bf16[28,448,128]{2,1,0:T(8,128)(2,1)} %param.15) | copy-start | bytes 9633796
  67.5 9.7 %copy-start.9 = (s32[4]{0:T(128)S(1)}, s32[4]{0:T(128)}, u32[]{:S(2)}) copy-start(s32[4]{0:T(128)} %param.28) | copy-start | bytes 52
  67.5 12.9 %collective-permute-start.1 = (f32[3072,128]{1,0:T(8,128)}, f32[3072,128]{1,0:T(8,128)}, u32[]{:S(2)}, u32[]{:S(2)}) collective-permute-start(f32[3072,128]{1,0:T(8,128)} %product.1.p1_ref), channel_id=1, source_target_pairs={{0,1},{1,0},{2,3},{3,2},{4,5},{5,4},{6,7},{7,6},{8,9},{9,8},{10,11... | collective-permute-start | bytes 4718600 | tf_op jit(solution)/shard_map/ppermute | solution.py:405
  69.3 14.9 %collective-permute-start.5 = (f32[64,16]{0,1:T(8,128)S(1)}, f32[64,16]{0,1:T(8,128)S(1)}, u32[]{:S(2)}, u32[]{:S(2)}) collective-permute-start(f32[64,16]{0,1:T(8,128)S(1)} %get-tuple-element.14), channel_id=1, source_target_pairs={{0,1},{1,2},{2,3},{3,4},{4,5},{5,6},{6,7},{7,8},{8,9},{9,10},{10,1... | collective-permute-start | bytes 12296 | tf_op jit(solution)/shard_map/ppermute | solution.py:28
  74.1 10.0 %collective-permute-start.6 = (f32[64,16]{0,1:T(8,128)S(1)}, f32[64,16]{0,1:T(8,128)S(1)}, u32[]{:S(2)}, u32[]{:S(2)}) collective-permute-start(f32[64,16]{0,1:T(8,128)S(1)} %get-tuple-element.15), channel_id=1, source_target_pairs={{1,0},{2,1},{3,2},{4,3},{5,4},{6,5},{7,6},{8,7},{9,8},{10,9},{11,1... | collective-permute-start | bytes 12296 | tf_op jit(solution)/shard_map/ppermute | solution.py:29
  81.7 11.5 %collective-permute-start.2 = (bf16[1024,128]{1,0:T(8,128)(2,1)S(1)}, bf16[1024,128]{1,0:T(8,128)(2,1)S(1)}, u32[]{:S(2)}, u32[]{:S(2)}) collective-permute-start(bf16[1024,128]{1,0:T(8,128)(2,1)S(1)} %fusion), channel_id=1, source_target_pairs={{2,0},{4,2},{6,4},{8,6},{10,8},{12,10},{14,12},{16,14},{18,16},{20... | collective-permute-start | bytes 786440 | tf_op jit(solution)/shard_map/ppermute | solution.py:408

commit v2 on v1

--- a/solution.py
+++ b/solution.py
@@ -11,6 +11,7 @@
 KW = 128
 HALO = 64
 SLOT = 32
+PART_SLOT = 16
 LANES = 128
 VMEM_LIMIT = 56 * 1024 * 1024
 MESH = pl.DeviceIdType.MESH
@@ -61,8 +62,8 @@
         row = step * rows + r
         for q in range(lane_tiles):
             cols = slice(q * LANES, (q + 1) * LANES)
-            a_acc[q, pl.ds(row, ch, stride=SLOT), :] = left[:, cols]
-            b_acc[q, pl.ds(row, ch, stride=SLOT), :] = right[:, cols]
+            a_acc[q, pl.ds(row, ch, stride=PART_SLOT), :] = left[:, cols]
+            b_acc[q, pl.ds(row, ch, stride=PART_SLOT), :] = right[:, cols]
 
     @pl.when(step == pl.num_programs(1) - 1)
     def _():
@@ -71,16 +72,16 @@
 
 
 def project(x, w, chunk):
-    tok_dev, span, width = x.shape
+    part, span, width = x.shape
     ch = w.shape[0] // 4
-    rows = 4
+    rows = part // 2
     tiles = -(-chunk // LANES)
-    shape = (tiles, ch * SLOT, LANES)
+    shape = (tiles, ch * PART_SLOT, LANES)
     out = jax.ShapeDtypeStruct((span // chunk,) + shape, jnp.bfloat16)
     out_spec = pl.BlockSpec((1,) + shape, lambda k, i: (k, 0, 0, 0))
     return pl.pallas_call(
         functools.partial(project_kernel, rows, chunk, tiles),
-        grid=(span // chunk, tok_dev // rows),
+        grid=(span // chunk, part // rows),
         in_specs=[
             pl.BlockSpec((rows, chunk, width), lambda k, i: (i, k, 0)),
             pl.BlockSpec(w.shape, lambda k, i: (0, 0)),
@@ -90,46 +91,45 @@
         scratch_shapes=[pltpu.VMEM(shape, jnp.float32)] * 2,
         compiler_params=pltpu.CompilerParams(vmem_limit_bytes=VMEM_LIMIT),
         cost_estimate=pl.CostEstimate(
-            flops=2 * x.size * 4 * ch, bytes_accessed=6 * x.size, transcendentals=2 * x.size
+            flops=2 * x.size * 4 * ch, bytes_accessed=16 * x.size, transcendentals=2 * x.size
         ),
         name="project",
     )(x, w)
 
 
-def product_kernel(ch, ao_ref, bo_ref, an_ref, bn_ref, out_ref):
+def product_kernel(ch, a0_ref, a1_ref, b0_ref, b1_ref, out_ref):
     quarter = ch // 4
-    half = ch // 2
-    tiles = ao_ref.shape[1]
+    tiles = a0_ref.shape[1]
 
     @pl.when(pl.program_id(0) == 0)
     def _():
         out_ref[...] = jnp.zeros_like(out_ref)
 
-    def load(ref, at):
-        return jnp.concatenate([ref[0, q, pl.ds(at, SLOT), :] for q in range(tiles)], axis=1)
+    def load(first, second, at):
+        rows = pl.ds(at, PART_SLOT)
+        return jnp.concatenate(
+            [
+                jnp.concatenate([ref[0, q, rows, :] for q in range(tiles)], axis=1)
+                for ref in (first, second)
+            ],
+            axis=0,
+        )
 
     def group(g, carry):
         outs = []
         for cl in range(4):
-            at = pl.multiple_of((cl * quarter + g) * SLOT, SLOT)
-            left = jnp.concatenate([load(ao_ref, at), load(an_ref, at)], axis=0)
-            right = jnp.concatenate([load(bo_ref, at), load(bn_ref, at)], axis=0)
-            outs.append(dot(left, right, NT))
-        first = pl.ds(pl.multiple_of(g * SLOT, SLOT), SLOT)
-        second = pl.ds(pl.multiple_of((quarter + g) * SLOT, SLOT), SLOT)
-        third = pl.ds(pl.multiple_of((half + g) * SLOT, SLOT), SLOT)
-        out_ref[first, :] += jnp.concatenate([outs[0][:SLOT], outs[2][:SLOT]], axis=1)
-        out_ref[second, :] += jnp.concatenate([outs[1][:SLOT], outs[3][:SLOT]], axis=1)
-        out_ref[third, :] += jnp.concatenate([o[SLOT:, :SLOT] for o in outs], axis=1)
+            at = pl.multiple_of((cl * quarter + g) * PART_SLOT, PART_SLOT)
+            outs.append(dot(load(a0_ref, a1_ref, at), load(b0_ref, b1_ref, at), NT))
+        out_ref[pl.ds(pl.multiple_of(g * SLOT, SLOT), SLOT), :] += jnp.concatenate(outs, axis=1)
         return carry
 
-    lax.fori_loop(0, quarter, group, 0)
-
-
-def product(own, low, ch):
-    chunks, tiles, rows, lanes = own[0].shape
+    lax.fori_loop(0, quarter, group, 0, unroll=4)
+
+
+def product(left, right, ch):
+    chunks, tiles, rows, lanes = left[0].shape
     spec = pl.BlockSpec((1, tiles, rows, lanes), lambda k: (k, 0, 0, 0))
-    out_rows = (ch // 2 + ch // 4) * SLOT
+    out_rows = ch // 4 * SLOT
     return pl.pallas_call(
         functools.partial(product_kernel, ch),
         grid=(chunks,),
@@ -137,44 +137,89 @@
         out_specs=pl.BlockSpec((out_rows, LANES), lambda k: (0, 0)),
         out_shape=jax.ShapeDtypeStruct((out_rows, LANES), jnp.float32),
         compiler_params=pltpu.CompilerParams(vmem_limit_bytes=VMEM_LIMIT),
+        cost_estimate=pl.CostEstimate(
+            flops=2 * SLOT * SLOT * ch * chunks * tiles * lanes,
+            bytes_accessed=16 * chunks * tiles * rows * lanes,
+            transcendentals=0,
+        ),
         name="product",
-    )(own[0], own[1], low[0], low[1])
-
-
-def tail_kernel(rows, tok_dev, ch, p1_ref, p2_ref, d_ref, band_ref, gate_ref, out_w_ref,
+    )(left[0], left[1], right[0], right[1])
+
+
+def gate_kernel(band_ref, gate_ref, out_ref):
+    rows, width, c = band_ref.shape
+    band = band_ref[...].reshape(rows * width, c)
+    gate = sigmoid(dot(normalize(band).astype(jnp.bfloat16), gate_ref[...]))
+    out_ref[...] = gate.reshape(rows, width, c)
+
+
+def gates_of(band, tri_gate):
+    tok_dev, width, c = band.shape
+    rows = 4
+    spec = pl.BlockSpec((rows, width, c), lambda i: (i, 0, 0))
+    return pl.pallas_call(
+        gate_kernel,
+        grid=(tok_dev // rows,),
+        in_specs=[spec, pl.BlockSpec(tri_gate.shape, lambda i: (0, 0))],
+        out_specs=spec,
+        out_shape=jax.ShapeDtypeStruct(band.shape, jnp.float32),
+        compiler_params=pltpu.CompilerParams(vmem_limit_bytes=VMEM_LIMIT),
+        cost_estimate=pl.CostEstimate(
+            flops=2 * band.size * c, bytes_accessed=16 * band.size, transcendentals=band.size
+        ),
+        name="gate",
+    )(band, tri_gate)
+
+
+def tail_kernel(rows, tok_dev, ch, own_ref, m1_ref, m2_ref, d_ref, band_ref, gate_ref, out_w_ref,
                 proj_ref, band_out_ref, table_ref):
     step = pl.program_id(0)
-    half, quarter = ch // 2, ch // 4
+    quarter = ch // 4
+    part = tok_dev // 2
     cp = proj_ref.shape[0]
+    width, c = band_ref.shape[1:]
 
     @pl.when(step == 0)
     def _():
         table_ref[...] = jnp.zeros_like(table_ref)
 
+    places, updates = [], []
     for r in range(rows):
         row = step * rows + r
-        near = pl.ds(row, half, stride=SLOT)
-        main = p1_ref[near, :] + p2_ref[near, :]
-        main = jnp.concatenate([main[:, :64], main[:, 64:]], axis=0)
-        above = d_ref[pl.ds(row, quarter, stride=SLOT), :]
-        above = jnp.concatenate([above[:, q * SLOT : (q + 1) * SLOT] for q in range(4)], axis=0)
-        prod = jnp.concatenate([main, above, above], axis=1)
+        row = row + jnp.where(row >= part, PART_SLOT - part, 0)
+        places.append(row)
+        near = pl.ds(row, quarter, stride=SLOT)
+        packed = [own_ref[near, :], m1_ref[near, :] + m2_ref[near, :], d_ref[near, :]]
+        prod = jnp.concatenate(
+            [
+                jnp.concatenate([p[:, q * SLOT : (q + 1) * SLOT] for p in packed], axis=1)
+                for q in range(4)
+            ],
+            axis=0,
+        )
         pn = normalize(prod, 0).astype(jnp.bfloat16)
-        update = dot(pn, out_w_ref[...], TN)
-        update = jnp.concatenate(
-            [update[SLOT : SLOT + tok_dev], update[:tok_dev], update[64 : 64 + tok_dev]], axis=0
-        )
-        band = band_ref[r].astype(jnp.float32)
-        gate = sigmoid(dot(normalize(band).astype(jnp.bfloat16), gate_ref[...]))
-        new = (band + gate * update).astype(jnp.bfloat16)
-        band_out_ref[r] = new
-        zt = normalize(new)
-        zt = jnp.concatenate([zt, jnp.zeros((LANES - 3 * tok_dev, zt.shape[1]), zt.dtype)], axis=0)
-        tok = dot(proj_ref[...], zt.astype(jnp.bfloat16), NT)
-        table_ref[pl.ds(row, cp, stride=SLOT), :] = tok
-
-
-def tail(p1, p2, d, band, tri_gate, tri_out, proj_t):
+        updates.append(dot(pn, out_w_ref[...], TN))
+    band = band_ref[...].reshape(rows * width, c).astype(jnp.float32)
+    gate = gate_ref[...].reshape(rows * width, c)
+    new = (band + gate * jnp.concatenate(updates, axis=0)).astype(jnp.bfloat16)
+    zt = normalize(new).astype(jnp.bfloat16)
+    lane = lax.broadcasted_iota(jnp.int32, (cp, width), 1)
+    used = lax.rem(lane, PART_SLOT) < part
+    plain = new.astype(jnp.float32)
+    for r in range(rows):
+        pieces = []
+        for slot in (1, 0, 2):
+            for half in range(2):
+                at = r * width + slot * SLOT + half * PART_SLOT
+                pieces.append(plain[at : at + part])
+        band_out_ref[r] = jnp.concatenate(pieces, axis=0).astype(jnp.bfloat16)
+        tok = dot(proj_ref[...], zt[r * width : (r + 1) * width], NT)
+        tok = jnp.where(used, tok, 0.0)
+        tok = jnp.concatenate([tok, jnp.zeros((cp, LANES - width), jnp.float32)], axis=1)
+        table_ref[pl.ds(places[r], cp, stride=SLOT), :] = tok
+
+
+def tail(own, m1, m2, d, band, gate, tri_out, proj_t):
     tok_dev, width, c = band.shape
     ch = tri_out.shape[0]
     cp = proj_t.shape[0]
@@ -184,16 +229,19 @@
     return pl.pallas_call(
         functools.partial(tail_kernel, rows, tok_dev, ch),
         grid=(tok_dev // rows,),
-        in_specs=[whole(p1), whole(p2), whole(d), band_spec, whole(tri_gate), whole(tri_out),
-                  whole(proj_t)],
-        out_specs=[band_spec, pl.BlockSpec((cp * SLOT, LANES), lambda i: (0, 0))],
+        in_specs=[whole(own), whole(m1), whole(m2), whole(d), band_spec, band_spec,
+                  whole(tri_out), whole(proj_t)],
+        out_specs=[
+            pl.BlockSpec((rows, 3 * tok_dev, c), lambda i: (i, 0, 0)),
+            pl.BlockSpec((cp * SLOT, LANES), lambda i: (0, 0)),
+        ],
         out_shape=[
-            jax.ShapeDtypeStruct(band.shape, jnp.bfloat16),
+            jax.ShapeDtypeStruct((tok_dev, 3 * tok_dev, c), jnp.bfloat16),
             jax.ShapeDtypeStruct((cp * SLOT, LANES), jnp.float32),
         ],
         compiler_params=pltpu.CompilerParams(vmem_limit_bytes=VMEM_LIMIT),
         name="tail",
-    )(p1, p2, d, band, tri_gate, tri_out, proj_t)
+    )(own, m1, m2, d, band, gate, tri_out, proj_t)
 
 
 def atom_kernel(devices, heads, blocks, mix_ref, table_ref, qtok_ref, ktok_ref, valid_ref,
@@ -397,19 +445,24 @@
     down = [(i + 1, i) for i in range(groups - 1)]
 
     half = tokens // 2
+    part = tok_dev // 2
     chunk = 8 * tok_dev
     own = lax.dynamic_slice_in_dim(pair, core * half, half, 1)
-    low = lax.ppermute(own, "tok", up)
+    low0 = lax.ppermute(own[:part], "tok", up)
+    low1 = lax.ppermute(own[part:], "tok", up)
     w = jnp.swapaxes(tri_in, 1, 2).reshape(4 * ch, -1)
-    partial = product(project(own, w, chunk), project(low, w, chunk), ch)
-    other = lax.ppermute(partial, "atm", [(0, 1), (1, 0)])
-    main_rows = ch // 2 * SLOT
-    back = (partial[main_rows:] + other[main_rows:]).astype(jnp.bfloat16)
-    back = lax.ppermute(back, "tok", down).astype(jnp.float32)
+    own0, own1 = project(own[:part], w, chunk), project(own[part:], w, chunk)
+    own_left, own_right = (own0[0], own1[0]), (own0[1], own1[1])
+    own_prod = product(own_left, own_right, ch)
+    own_prod = own_prod + lax.ppermute(own_prod, "atm", [(0, 1), (1, 0)])
 
     padded = jnp.pad(pair, ((0, 0), (tok_dev, tok_dev), (0, 0)))
     band = lax.dynamic_slice_in_dim(padded, shard * tok_dev, 3 * tok_dev, 1)
-    pair_band, table = tail(partial, other, back, band, tri_gate, tri_out, pair_proj.T)
+    band = band.reshape(tok_dev, 3, 2, part, -1)
+    band = jnp.concatenate([band[:, 1:2], band[:, 0:1], band[:, 2:3]], axis=1)
+    band = jnp.pad(band, ((0, 0), (0, 0), (0, 0), (0, PART_SLOT - part), (0, 0)))
+    band = band.reshape(tok_dev, 3 * SLOT, -1)
+    gate = gates_of(band, tri_gate)
 
     atoms = atom_act.shape[0]
     heads = bias_proj.shape[2]
@@ -425,15 +478,48 @@
     mixed = jnp.dot(
         pair_mlp.astype(jnp.float32), projections, precision=lax.Precision.HIGHEST
     )
-    atoms_out = atoms_part(
+    spread = PART_SLOT - part
+    qtok = atom_token - shard * tok_dev
+    qtok = qtok + jnp.where(qtok >= part, spread, 0)
+    ktok = labels_ext[:, 0] - (shard - 1) * tok_dev
+    kgroup = (ktok >= tok_dev).astype(jnp.int32) + (ktok >= 2 * tok_dev).astype(jnp.int32)
+    ktok = ktok - kgroup * tok_dev
+    ktok = ktok + jnp.where(ktok >= part, spread, 0)
+    ktok = ktok + SLOT * jnp.where(kgroup == 0, 1, jnp.where(kgroup == 1, 0, 2))
+    early = (
         jnp.concatenate([projections, mixed], 0),
-        table,
-        (atom_token - shard * tok_dev)[:, None],
-        (labels_ext[:, 0] - (shard - 1) * tok_dev)[None, :],
+        qtok[:, None],
+        ktok[None, :],
         labels_ext[:, 1][None, :],
         jnp.repeat(offsets, QUERY_ATOMS)[:, None],
         query_term,
         key_term_ext.T,
+        band,
+        gate,
+        own_prod,
+        pair_proj.T,
+    )
+    low1, early = lax.optimization_barrier((low1, early))
+    mix, qtok, ktok, valid, offset, cq, ck, band, gate, own_prod, proj_t = early
+
+    low0, low1 = project(low0, w, chunk), project(low1, w, chunk)
+    low_left, low_right = (low0[0], low1[0]), (low0[1], low1[1])
+    swap = [(0, 1), (1, 0)]
+    back = product(low_left, own_right, ch)
+    back = (back + lax.ppermute(back, "atm", swap)).astype(jnp.bfloat16)
+    main = product(own_left, low_right, ch)
+    other = lax.ppermute(main, "atm", swap)
+    back = lax.ppermute(back, "tok", down).astype(jnp.float32)
+    pair_band, table = tail(own_prod, main, other, back, band, gate, tri_out, proj_t)
+    atoms_out = atoms_part(
+        mix,
+        table,
+        qtok,
+        ktok,
+        valid,
+        offset,
+        cq,
+        ck,
         atom_act,
         atom_cond,
         block_weights,

time: 129 us -> 125 us (0.969)
  waiting for transfers between devices: 21.9 us -> 11.2 us
  local copies, waits for them, and re-layouts: 6.63 us -> 11.3 us
  starting transfers between devices: 19.2 us -> 22.1 us
  Pallas kernels: 74.2 us -> 71.9 us
  other arithmetic: 4.09 us -> 5.78 us
    ppermute x2 -> x5, waiting for transfers between devices: 13.6 us -> 0.01 us  [the longest x1 0.01 us: local(): low1 = lax.ppermute(own[part:], 'tok', up)]
    pallas_call x0 -> x1, Pallas kernels: none -> 5.9 us  [gates_of(): pl.pallas_call(gate_kernel, grid=(tok_dev // rows,), in_specs=[spec, pl.B...]
    pallas_call x2 -> x4, Pallas kernels: 29 us -> 23.3 us  [project(): pl.pallas_call(functools.partial(project_kernel, rows, chunk, tiles), gri...]
    pallas_call x1, Pallas kernels: 14.5 us -> 8.78 us  [tail(): pl.pallas_call(functools.partial(tail_kernel, rows, tok_dev, ch), grid=(t...]
    ppermute x2, waiting for transfers between devices: 0.01 us -> 3.71 us  [with_halo(): after = lax.ppermute(leading, axis, down)]
    pallas_call x1 -> x3, Pallas kernels: 12.7 us -> 16.1 us  [product(): pl.pallas_call(functools.partial(product_kernel, ch), grid=(chunks,), in_...]
    ppermute x2 -> x5, starting transfers between devices: 4.68 us -> 7.95 us  [the longest x1 3.12 us: local(): low0 = lax.ppermute(own[:part], 'tok', up)]
    slice x0 -> x2, local copies, waits for them, and re-layouts: none -> 2.8 us  [the longest x1 2.71 us: local(): own0, own1 = (project(own[:part], w, chunk), project(own[part:], w, chunk))]
  transfers between devices with their start and end apart: 7 -> 10, of which waited for: 2 -> 2; matrix products, arithmetic and copies ran while one was open for 6% -> 10% of each run, Pallas kernels for 33% -> 28%
where the time goes in v2:
time: 125 us; the launch traced here: 124 us
  Pallas kernels  71.9 us (58%)
  starting transfers between devices  22.1 us (18%)
  local copies, waits for them, and re-layouts  11.3 us (9%)
  waiting for transfers between devices  11.2 us (9%)
  other arithmetic  5.78 us (5%)
    pallas_call x4, Pallas kernels, project(): pl.pallas_call(functools.partial(project_kernel, rows, chunk, tiles), gri...  23.3 us
    pallas_call x1, Pallas kernels, atoms_part(): pl.pallas_call(functools.partial(atom_kernel, devices, heads, blocks), in...  17.9 us
    pallas_call x3, Pallas kernels, product(): pl.pallas_call(functools.partial(product_kernel, ch), grid=(chunks,), in_...  16.1 us
    pallas_call x1, Pallas kernels, tail(): pl.pallas_call(functools.partial(tail_kernel, rows, tok_dev, ch), grid=(t...  8.78 us
    ppermute x2, starting transfers between devices, with_halo(): before = lax.ppermute(last, axis, up)  8.43 us
    ppermute x1, waiting for transfers between devices, local(): back = lax.ppermute(back, 'tok', down).astype(jnp.float32)  7.48 us
    pallas_call x1, Pallas kernels, gates_of(): pl.pallas_call(gate_kernel, grid=(tok_dev // rows,), in_specs=[spec, pl.B...  5.9 us
    ppermute x2, starting transfers between devices, with_halo(): after = lax.ppermute(leading, axis, down)  3.84 us
  transfers between devices with their start and end apart: 10, of which 2 were waited for; matrix products, arithmetic and copies ran while one was open for 10% of the time, Pallas kernels for 28%

profile of v2, /device:TPU:23, one launch (start us, length us, event | category | flops | bytes accessed | tf_op | source)
XLA Modules:
  0.0 123.6 jit_solution(15721130326235470017)
XLA Ops:
  0.7 2.7 %constant_dynamic-slice_fusion.1 = (bf16[14,224,128]{2,1,0:T(8,128)(2,1)}, bf16[14,224,128]{2,1,0:T(8,128)(2,1)}) fusion(bf16[28,448,128]{2,1,0:T(8,128)(2,1)} %param.15, s32[]{:T(128)S(6)} %select_n.42, s32[]{:T(128)S(6)} %add.70), kind=kLoop, calls=%fused_computation.37 | loop fusion | bytes 3211272 | tf_op jit(solution)/shard_map/slice | solution.py:454
  3.4 3.1 %collective-permute-start = (bf16[14,224,128]{2,1,0:T(8,128)(2,1)}, bf16[14,224,128]{2,1,0:T(8,128)(2,1)}, u32[]{:S(2)}, u32[]{:S(2)}) collective-permute-start(bf16[14,224,128]{2,1,0:T(8,128)(2,1)} %get-tuple-element.47.x_ref), channel_id=1, source_target_pairs={{0,2},{2,4},{4,6},{6,8},{8,10},{10,12},{12,14},{14,16},{16,18},{18... | collective-permute-start | bytes 2408456 | tf_op jit(solution)/shard_map/ppermute | solution.py:452
  6.5 3.1 %collective-permute-start.6 = (bf16[14,224,128]{2,1,0:T(8,128)(2,1)}, bf16[14,224,128]{2,1,0:T(8,128)(2,1)}, u32[]{:S(2)}, u32[]{:S(2)}) collective-permute-start(bf16[14,224,128]{2,1,0:T(8,128)(2,1)} %get-tuple-element.46.x_ref), channel_id=1, source_target_pairs={{0,2},{2,4},{4,6},{6,8},{8,10},{10,12},{12,14},{14,16},{16,18},{18... | collective-permute-start | bytes 2408456 | tf_op jit(solution)/shard_map/ppermute | solution.py:451
  9.6 0.8 copy.24
  10.4 5.8 %project.4 = (bf16[1,2,2048,128]{3,2,1,0:T(8,128)(2,1)}, bf16[1,2,2048,128]{3,2,1,0:T(8,128)(2,1)}) custom-call(bf16[14,224,128]{2,1,0:T(8,128)(2,1)} %get-tuple-element.46.x_ref, bf16[512,128]{1,0:T(8,128)(2,1)} %bitcast.30), custom_call_target="tpu_custom_call" | custom-call | flops 411041792 | bytes 6422528 | tf_op jit(solution)/shard_map/project/pallas_call | solution.py:82
  16.2 5.8 %project.5 = (bf16[1,2,2048,128]{3,2,1,0:T(8,128)(2,1)}, bf16[1,2,2048,128]{3,2,1,0:T(8,128)(2,1)}) custom-call(bf16[14,224,128]{2,1,0:T(8,128)(2,1)} %get-tuple-element.47.x_ref, bf16[512,128]{1,0:T(8,128)(2,1)} %bitcast.31), custom_call_target="tpu_custom_call" | custom-call | flops 411041792 | bytes 6422528 | tf_op jit(solution)/shard_map/project/pallas_call | solution.py:82
  22.1 5.5 %product.3 = f32[1024,128]{1,0:T(8,128)} custom-call(bf16[1,2,2048,128]{3,2,1,0:T(8,128)(2,1)} %get-tuple-element.24.a0_ref, bf16[1,2,2048,128]{3,2,1,0:T(8,128)(2,1)} %get-tuple-element.25.a1_ref, bf16[1,2,2048,128]{3,2,1,0:T(8,128)(2,1)} %get-tuple-element.26.b0_ref, bf16[1,2,2048,128]{3,2,1,0:T(8,128)(2,1)} %get-tuple-element.27.b1_ref), custom_call_target="tpu_custom_call" | custom-call | flops 67108864 | bytes 8388608 | tf_op jit(solution)/shard_map/product/pallas_call | solution.py:133
  27.5 1.2 %collective-permute-start.5 = (f32[1024,128]{1,0:T(8,128)}, f32[1024,128]{1,0:T(8,128)}, u32[]{:S(2)}, u32[]{:S(2)}) collective-permute-start(f32[1024,128]{1,0:T(8,128)} %product.3), channel_id=1, source_target_pairs={{0,1},{1,0},{2,3},{3,2},{4,5},{5,4},{6,7},{7,6},{8,9},{9,8},{10,11... | collective-permute-start | bytes 1572872 | tf_op jit(solution)/shard_map/ppermute | solution.py:457
  28.8 0.1 fusion.26
  28.9 3.0 %collective-permute-start.1 = (s32[64,2]{0,1:T(2,128)S(1)}, s32[64,2]{0,1:T(2,128)S(1)}, u32[]{:S(2)}, u32[]{:S(2)}) collective-permute-start(s32[64,2]{0,1:T(2,128)S(1)} %get-tuple-element.53), channel_id=1, source_target_pairs={{0,1},{1,2},{2,3},{3,4},{4,5},{5,6},{6,7},{7,8},{8,9},{9,10},{10,1... | collective-permute-start | bytes 1544 | tf_op jit(solution)/shard_map/ppermute | solution.py:29
  31.9 1.9 %collective-permute-start.2 = (s32[64,2]{0,1:T(2,128)S(1)}, s32[64,2]{0,1:T(2,128)S(1)}, u32[]{:S(2)}, u32[]{:S(2)}) collective-permute-start(s32[64,2]{0,1:T(2,128)S(1)} %get-tuple-element.54), channel_id=1, source_target_pairs={{1,0},{2,1},{3,2},{4,3},{5,4},{6,5},{7,6},{8,7},{9,8},{10,9},{11,1... | collective-permute-start | bytes 1544 | tf_op jit(solution)/shard_map/ppermute | solution.py:30
  33.8 0.1 fusion.5
  34.0 0.1 fusion.7
  34.1 1.1 pad_dynamic-slice_fusion
  35.2 1.3 %reshape.77 = bf16[28,3,2,14,128]{4,3,2,1,0:T(8,128)(2,1)S(1)} reshape(bf16[28,84,128]{2,1,0:T(8,128)(2,1)} %pad_dynamic-slice_fusion) | data formatting | bytes 1204224 | tf_op jit(solution)/shard_map/reshape | solution.py:461
  36.5 0.1 fusion.24
  36.6 0.1 fusion.25
  36.7 0.1 fusion.27
  36.8 1.1 fusion.4
  37.9 0.1 copy.22
  38.0 0.6 pad_maximum_fusion.mix_ref
  38.6 5.9 %gate.1.gate_ref = f32[28,96,128]{2,1,0:T(8,128)} custom-call(bf16[28,96,128]{2,1,0:T(8,128)(2,1)} %bitcast.27, bf16[128,128]{1,0:T(8,128)(2,1)} %gate_ref.1), custom_call_target="tpu_custom_call" | custom-call | flops 88080384 | bytes 5505024 | tf_op jit(solution)/shard_map/gate/pallas_call | solution.py:160
  44.5 0.1 broadcast_in_dim.35
  44.6 0.1 broadcast_in_dim_reshape.3
  44.7 5.4 %collective-permute-start.3 = (f32[64,16]{0,1:T(8,128)S(1)}, f32[64,16]{0,1:T(8,128)S(1)}, u32[]{:S(2)}, u32[]{:S(2)}) collective-permute-start(f32[64,16]{0,1:T(8,128)S(1)} %get-tuple-element.51), channel_id=1, source_target_pairs={{0,1},{1,2},{2,3},{3,4},{4,5},{5,6},{6,7},{7,8},{8,9},{9,10},{10,1... | collective-permute-start | bytes 12296 | tf_op jit(solution)/shard_map/ppermute | solution.py:29
  50.1 1.9 %collective-permute-start.4 = (f32[64,16]{0,1:T(8,128)S(1)}, f32[64,16]{0,1:T(8,128)S(1)}, u32[]{:S(2)}, u32[]{:S(2)}) collective-permute-start(f32[64,16]{0,1:T(8,128)S(1)} %get-tuple-element.52), channel_id=1, source_target_pairs={{1,0},{2,1},{3,2},{4,3},{5,4},{6,5},{7,6},{8,7},{9,8},{10,9},{11,1... | collective-permute-start | bytes 12296 | tf_op jit(solution)/shard_map/ppermute | solution.py:30
  52.0 0.1 pad_add_fusion
  52.1 0.5 slice_bitcast_fusion.valid_ref
  52.6 0.5 fusion.16.ktok_ref
  53.2 3.7 %collective-permute-done.4 = f32[64,16]{0,1:T(8,128)S(1)} collective-permute-done((f32[64,16]{0,1:T(8,128)S(1)}, f32[64,16]{0,1:T(8,128)S(1)}, u32[]{:S(2)}, u32[]{:S(2)}) %collective-permute-start.4) | collective-permute-done | bytes 4128 | tf_op jit(solution)/shard_map/ppermute | solution.py:30
  56.9 0.7 maximum_bitcast_fusion.ck_ref
  57.6 1.9 %add.64.own_ref = f32[1024,128]{1,0:T(8,128)} add(f32[1024,128]{1,0:T(8,128)S(1)} %copy-done.2, f32[1024,128]{1,0:T(8,128)} %collective-permute-done.5) | non-fusion elementwise | flops 131072 | bytes 1572864 | tf_op jit(solution)/shard_map/add | solution.py:457
  59.5 5.8 %project.7 = (bf16[1,2,2048,128]{3,2,1,0:T(8,128)(2,1)}, bf16[1,2,2048,128]{3,2,1,0:T(8,128)(2,1)}) custom-call(bf16[14,224,128]{2,1,0:T(8,128)(2,1)} %collective-permute-done.x_ref, bf16[512,128]{1,0:T(8,128)(2,1)} %bitcast.32), custom_call_target="tpu_custom_call" | custom-call | flops 411041792 | bytes 6422528 | tf_op jit(solution)/shard_map/project/pallas_call | solution.py:82
  65.3 5.8 %project.6 = (bf16[1,2,2048,128]{3,2,1,0:T(8,128)(2,1)}, bf16[1,2,2048,128]{3,2,1,0:T(8,128)(2,1)}) custom-call(bf16[14,224,128]{2,1,0:T(8,128)(2,1)} %collective-permute-done.6.x_ref, bf16[512,128]{1,0:T(8,128)(2,1)} %bitcast.33), custom_call_target="tpu_custom_call" | custom-call | flops 411041792 | bytes 6422528 | tf_op jit(solution)/shard_map/project/pallas_call | solution.py:82
  71.1 5.2 %product.5 = f32[1024,128]{1,0:T(8,128)} custom-call(bf16[1,2,2048,128]{3,2,1,0:T(8,128)(2,1)} %get-tuple-element.32.a0_ref, bf16[1,2,2048,128]{3,2,1,0:T(8,128)(2,1)} %get-tuple-element.33.a1_ref, bf16[1,2,2048,128]{3,2,1,0:T(8,128)(2,1)} %get-tuple-element.26.b0_ref, bf16[1,2,2048,128]{3,2,1,0:T(8,128)(2,1)} %get-tuple-element.27.b1_ref), custom_call_target="tpu_custom_call" | custom-call | flops 67108864 | bytes 8388608 | tf_op jit(solution)/shard_map/product/pallas_call | solution.py:133
  76.4 5.3 %product.4.m1_ref = f32[1024,128]{1,0:T(8,128)} custom-call(bf16[1,2,2048,128]{3,2,1,0:T(8,128)(2,1)} %get-tuple-element.24.a0_ref, bf16[1,2,2048,128]{3,2,1,0:T(8,128)(2,1)} %get-tuple-element.25.a1_ref, bf16[1,2,2048,128]{3,2,1,0:T(8,128)(2,1)} %get-tuple-element.29.b0_ref, bf16[1,2,2048,128]{3,2,1,0:T(8,128)(2,1)} %get-tuple-element.31.b1_ref), custom_call_target="tpu_custom_call" | custom-call | flops 67108864 | bytes 8388608 | tf_op jit(solution)/shard_map/product/pallas_call | solution.py:133
  81.7 0.5 collective-permute-start.7
  82.2 0.1 add_convert_fusion
  82.3 1.9 %collective-permute-start.9 = (bf16[1024,128]{1,0:T(8,128)(2,1)S(1)}, bf16[1024,128]{1,0:T(8,128)(2,1)S(1)}, u32[]{:S(2)}, u32[]{:S(2)}) collective-permute-start(bf16[1024,128]{1,0:T(8,128)(2,1)S(1)} %add_convert_fusion), channel_id=1, source_target_pairs={{2,0},{4,2},{6,4},{8,6},{10,8},{12,10},{14,12},{16,14},{18,16},{20... | collective-permute-start | bytes 786440 | tf_op jit(solution)/shard_map/ppermute | solution.py:512
  84.2 0.7 copy.25.qtok_ref
  84.9 0.7 copy.26.offset_ref
  85.7 0.7 copy.27.cq_ref
  86.4 7.5 %collective-permute-done.9 = bf16[1024,128]{1,0:T(8,128)(2,1)S(1)} collective-permute-done((bf16[1024,128]{1,0:T(8,128)(2,1)S(1)}, bf16[1024,128]{1,0:T(8,128)(2,1)S(1)}, u32[]{:S(2)}, u32[]{:S(2)}) %collective-permute-start.9) | collective-permute-done | bytes 262176 | tf_op jit(solution)/shard_map/ppermute | solution.py:512
  93.9 0.8 convert_element_type.38.d_ref
  94.7 0.8 copy-done.4
  95.5 8.8 %tail.1 = (bf16[28,84,128]{2,1,0:T(8,128)(2,1)}, f32[512,128]{1,0:T(8,128)}) custom-call(f32[1024,128]{1,0:T(8,128)} %add.64.own_ref, f32[1024,128]{1,0:T(8,128)} %product.4.m1_ref, f32[1024,128]{1,0:T(8,128)} %copy-done.4, f32[1024,128]{1,0:T(8,128)} %convert_element_type.38.d_ref, bf16[28,96,128]{2,1,0:T(8,128)(2,1)} %bitcast.28, ...), custom_call_target="tpu_custom_call" | custom-call | tf_op jit(solution)/shard_map/tail/pallas_call | solution.py:229
  104.3 17.9 %atoms.1 = bf16[128,128]{1,0:T(8,128)(2,1)} custom-call(f32[32,12]{1,0:T(8,128)} %pad_maximum_fusion.mix_ref, f32[512,128]{1,0:T(8,128)} %get-tuple-element.39.table_ref, s32[128,1]{1,0:T(8,128)} %copy.25.qtok_ref, s32[1,256]{1,0:T(1,128)} %fusion.16.ktok_ref, s32[1,256]{1,0:T(1,128)} %slice_bitcast_fusion.valid_ref, s32[128,1]{1,0:T(8,128)} %copy.26.offset_ref, ...), custom_call_target="tpu_custom_call" | custom-call | tf_op jit(solution)/shard_map/atoms/pallas_call | solution.py:403
  122.2 1.4 %copy.30 = bf16[128,128]{1,0:T(8,128)(2,1)} copy(bf16[128,128]{1,0:T(8,128)(2,1)} %atoms.1) | data formatting | bytes 65536
  (37 shorter events, 0.1 us)
Async XLA Ops:
  0.6 36.1 %copy-start = (bf16[16,16]{1,0:T(8,128)(2,1)S(1)}, bf16[16,16]{1,0:T(8,128)(2,1)}, u32[]{:S(2)}) copy-start(bf16[16,16]{1,0:T(8,128)(2,1)} %param.23) | copy-start | bytes 1540
  0.7 9.0 %copy-start.6 = (bf16[4,128,128]{2,1,0:T(8,128)(2,1)S(1)}, bf16[4,128,128]{2,1,0:T(8,128)(2,1)}, u32[]{:S(2)}) copy-start(bf16[4,128,128]{2,1,0:T(8,128)(2,1)} %param.16) | copy-start | bytes 393220
  3.4 56.1 %collective-permute-start = (bf16[14,224,128]{2,1,0:T(8,128)(2,1)}, bf16[14,224,128]{2,1,0:T(8,128)(2,1)}, u32[]{:S(2)}, u32[]{:S(2)}) collective-permute-start(bf16[14,224,128]{2,1,0:T(8,128)(2,1)} %get-tuple-element.47.x_ref), channel_id=1, source_target_pairs={{0,2},{2,4},{4,6},{6,8},{8,10},{10,12},{12,14},{14,16},{16,18},{18... | collective-permute-start | bytes 2408456 | tf_op jit(solution)/shard_map/ppermute | solution.py:452
  6.5 58.8 %collective-permute-start.6 = (bf16[14,224,128]{2,1,0:T(8,128)(2,1)}, bf16[14,224,128]{2,1,0:T(8,128)(2,1)}, u32[]{:S(2)}, u32[]{:S(2)}) collective-permute-start(bf16[14,224,128]{2,1,0:T(8,128)(2,1)} %get-tuple-element.46.x_ref), channel_id=1, source_target_pairs={{0,2},{2,4},{4,6},{6,8},{8,10},{10,12},{12,14},{14,16},{16,18},{18... | collective-permute-start | bytes 2408456 | tf_op jit(solution)/shard_map/ppermute | solution.py:451
  22.0 6.7 %copy-start.9 = (s32[128]{0:T(128)S(1)}, s32[128]{0:T(128)}, u32[]{:S(2)}) copy-start(s32[128]{0:T(128)} %param.26) | copy-start | bytes 1540
  22.0 6.7 %copy-start.10 = (s32[128]{0:T(128)S(1)}, s32[128]{0:T(128)}, u32[]{:S(2)}) copy-start(s32[128]{0:T(128)} %param.27) | copy-start | bytes 1540
  22.0 11.8 %copy-start.5 = (bf16[128,128]{1,0:T(8,128)(2,1)S(1)}, bf16[128,128]{1,0:T(8,128)(2,1)}, u32[]{:S(2)}) copy-start(bf16[128,128]{1,0:T(8,128)(2,1)} %cond_ref.1) | copy-start | bytes 98308
  22.1 11.8 %copy-start.7 = (bf16[2,128,16]{1,2,0:T(8,128)(2,1)S(1)}, bf16[2,128,16]{1,2,0:T(8,128)(2,1)}, u32[]{:S(2)}) copy-start(bf16[2,128,16]{1,2,0:T(8,128)(2,1)} %param.22) | copy-start | bytes 24580
  22.1 12.1 %copy-start.1 = (bf16[28,448,128]{2,1,0:T(8,128)(2,1)S(1)}, bf16[28,448,128]{2,1,0:T(8,128)(2,1)}, u32[]{:S(2)}) copy-start(bf16[28,448,128]{2,1,0:T(8,128)(2,1)} %param.15) | copy-start | bytes 9633796
  27.5 30.0 %collective-permute-start.5 = (f32[1024,128]{1,0:T(8,128)}, f32[1024,128]{1,0:T(8,128)}, u32[]{:S(2)}, u32[]{:S(2)}) collective-permute-start(f32[1024,128]{1,0:T(8,128)} %product.3), channel_id=1, source_target_pairs={{0,1},{1,0},{2,3},{3,2},{4,5},{5,4},{6,7},{7,6},{8,9},{9,8},{10,11... | collective-permute-start | bytes 1572872 | tf_op jit(solution)/shard_map/ppermute | solution.py:457
  28.9 15.8 %collective-permute-start.1 = (s32[64,2]{0,1:T(2,128)S(1)}, s32[64,2]{0,1:T(2,128)S(1)}, u32[]{:S(2)}, u32[]{:S(2)}) collective-permute-start(s32[64,2]{0,1:T(2,128)S(1)} %get-tuple-element.53), channel_id=1, source_target_pairs={{0,1},{1,2},{2,3},{3,4},{4,5},{5,6},{6,7},{7,8},{8,9},{9,10},{10,1... | collective-permute-start | bytes 1544 | tf_op jit(solution)/shard_map/ppermute | solution.py:29
  31.9 18.2 %collective-permute-start.2 = (s32[64,2]{0,1:T(2,128)S(1)}, s32[64,2]{0,1:T(2,128)S(1)}, u32[]{:S(2)}, u32[]{:S(2)}) collective-permute-start(s32[64,2]{0,1:T(2,128)S(1)} %get-tuple-element.54), channel_id=1, source_target_pairs={{1,0},{2,1},{3,2},{4,3},{5,4},{6,5},{7,6},{8,7},{9,8},{10,9},{11,1... | collective-permute-start | bytes 1544 | tf_op jit(solution)/shard_map/ppermute | solution.py:30
  35.2 1.5 %copy-start.8 = (bf16[3,16,4]{1,2,0:T(4,128)(2,1)S(1)}, bf16[3,16,4]{1,2,0:T(4,128)(2,1)}, u32[]{:S(2)}) copy-start(bf16[3,16,4]{1,2,0:T(4,128)(2,1)} %param.24) | copy-start | bytes 1156
  35.2 1.5 %copy-start.11 = (s32[4]{0:T(128)S(1)}, s32[4]{0:T(128)}, u32[]{:S(2)}) copy-start(s32[4]{0:T(128)} %param.28) | copy-start | bytes 52
  37.9 19.7 %copy-start.2 = (f32[1024,128]{1,0:T(8,128)S(1)}, f32[1024,128]{1,0:T(8,128)}, u32[]{:S(2)}) copy-start(f32[1024,128]{1,0:T(8,128)} %product.3) | copy-start | bytes 1572868
  44.7 8.5 %collective-permute-start.3 = (f32[64,16]{0,1:T(8,128)S(1)}, f32[64,16]{0,1:T(8,128)S(1)}, u32[]{:S(2)}, u32[]{:S(2)}) collective-permute-start(f32[64,16]{0,1:T(8,128)S(1)} %get-tuple-element.51), channel_id=1, source_target_pairs={{0,1},{1,2},{2,3},{3,4},{4,5},{5,6},{6,7},{7,8},{8,9},{9,10},{10,1... | collective-permute-start | bytes 12296 | tf_op jit(solution)/shard_map/ppermute | solution.py:29
  50.1 6.8 %collective-permute-start.4 = (f32[64,16]{0,1:T(8,128)S(1)}, f32[64,16]{0,1:T(8,128)S(1)}, u32[]{:S(2)}, u32[]{:S(2)}) collective-permute-start(f32[64,16]{0,1:T(8,128)S(1)} %get-tuple-element.52), channel_id=1, source_target_pairs={{1,0},{2,1},{3,2},{4,3},{5,4},{6,5},{7,6},{8,7},{9,8},{10,9},{11,1... | collective-permute-start | bytes 12296 | tf_op jit(solution)/shard_map/ppermute | solution.py:30
  76.4 5.8 %collective-permute-start.8 = (f32[1024,128]{1,0:T(8,128)}, f32[1024,128]{1,0:T(8,128)S(1)}, u32[]{:S(2)}, u32[]{:S(2)}) collective-permute-start(f32[1024,128]{1,0:T(8,128)} %product.5), channel_id=1, source_target_pairs={{0,1},{1,0},{2,3},{3,2},{4,5},{5,4},{6,7},{7,6},{8,9},{9,8},{10,11... | collective-permute-start | bytes 1572872 | tf_op jit(solution)/shard_map/ppermute | solution.py:509
  76.4 5.8 %copy-start.3 = (f32[1024,128]{1,0:T(8,128)S(1)}, f32[1024,128]{1,0:T(8,128)}, u32[]{:S(2)}) copy-start(f32[1024,128]{1,0:T(8,128)} %product.5) | copy-start | bytes 1572868
  81.7 13.0 %collective-permute-start.7 = (f32[1024,128]{1,0:T(8,128)}, f32[1024,128]{1,0:T(8,128)S(1)}, u32[]{:S(2)}, u32[]{:S(2)}) collective-permute-start(f32[1024,128]{1,0:T(8,128)} %product.4.m1_ref), channel_id=1, source_target_pairs={{0,1},{1,0},{2,3},{3,2},{4,5},{5,4},{6,7},{7,6},{8,9},{9,8},{10,11... | collective-permute-start | bytes 1572872 | tf_op jit(solution)/shard_map/ppermute | solution.py:511
  82.3 11.6 %collective-permute-start.9 = (bf16[1024,128]{1,0:T(8,128)(2,1)S(1)}, bf16[1024,128]{1,0:T(8,128)(2,1)S(1)}, u32[]{:S(2)}, u32[]{:S(2)}) collective-permute-start(bf16[1024,128]{1,0:T(8,128)(2,1)S(1)} %add_convert_fusion), channel_id=1, source_target_pairs={{2,0},{4,2},{6,4},{8,6},{10,8},{12,10},{14,12},{16,14},{18,16},{20... | collective-permute-start | bytes 786440 | tf_op jit(solution)/shard_map/ppermute | solution.py:512
  94.7 0.8 copy-start.4

commit v3 on v2

--- a/solution.py
+++ b/solution.py
@@ -11,7 +11,6 @@
 KW = 128
 HALO = 64
 SLOT = 32
-PART_SLOT = 16
 LANES = 128
 VMEM_LIMIT = 56 * 1024 * 1024
 MESH = pl.DeviceIdType.MESH
@@ -62,8 +61,8 @@
         row = step * rows + r
         for q in range(lane_tiles):
             cols = slice(q * LANES, (q + 1) * LANES)
-            a_acc[q, pl.ds(row, ch, stride=PART_SLOT), :] = left[:, cols]
-            b_acc[q, pl.ds(row, ch, stride=PART_SLOT), :] = right[:, cols]
+            a_acc[q, pl.ds(row, ch, stride=SLOT), :] = left[:, cols]
+            b_acc[q, pl.ds(row, ch, stride=SLOT), :] = right[:, cols]
 
     @pl.when(step == pl.num_programs(1) - 1)
     def _():
@@ -74,9 +73,9 @@
 def project(x, w, chunk):
     part, span, width = x.shape
     ch = w.shape[0] // 4
-    rows = part // 2
+    rows = part // 4
     tiles = -(-chunk // LANES)
-    shape = (tiles, ch * PART_SLOT, LANES)
+    shape = (tiles, ch * SLOT, LANES)
     out = jax.ShapeDtypeStruct((span // chunk,) + shape, jnp.bfloat16)
     out_spec = pl.BlockSpec((1,) + shape, lambda k, i: (k, 0, 0, 0))
     return pl.pallas_call(
@@ -97,29 +96,22 @@
     )(x, w)
 
 
-def product_kernel(ch, a0_ref, a1_ref, b0_ref, b1_ref, out_ref):
+def product_kernel(ch, a_ref, b_ref, out_ref):
     quarter = ch // 4
-    tiles = a0_ref.shape[1]
+    tiles = a_ref.shape[1]
 
     @pl.when(pl.program_id(0) == 0)
     def _():
         out_ref[...] = jnp.zeros_like(out_ref)
 
-    def load(first, second, at):
-        rows = pl.ds(at, PART_SLOT)
-        return jnp.concatenate(
-            [
-                jnp.concatenate([ref[0, q, rows, :] for q in range(tiles)], axis=1)
-                for ref in (first, second)
-            ],
-            axis=0,
-        )
+    def load(ref, at):
+        return jnp.concatenate([ref[0, q, pl.ds(at, SLOT), :] for q in range(tiles)], axis=1)
 
     def group(g, carry):
         outs = []
         for cl in range(4):
-            at = pl.multiple_of((cl * quarter + g) * PART_SLOT, PART_SLOT)
-            outs.append(dot(load(a0_ref, a1_ref, at), load(b0_ref, b1_ref, at), NT))
+            at = pl.multiple_of((cl * quarter + g) * SLOT, SLOT)
+            outs.append(dot(load(a_ref, at), load(b_ref, at), NT))
         out_ref[pl.ds(pl.multiple_of(g * SLOT, SLOT), SLOT), :] += jnp.concatenate(outs, axis=1)
         return carry
 
@@ -127,13 +119,13 @@
 
 
 def product(left, right, ch):
-    chunks, tiles, rows, lanes = left[0].shape
+    chunks, tiles, rows, lanes = left.shape
     spec = pl.BlockSpec((1, tiles, rows, lanes), lambda k: (k, 0, 0, 0))
     out_rows = ch // 4 * SLOT
     return pl.pallas_call(
         functools.partial(product_kernel, ch),
         grid=(chunks,),
-        in_specs=[spec] * 4,
+        in_specs=[spec] * 2,
         out_specs=pl.BlockSpec((out_rows, LANES), lambda k: (0, 0)),
         out_shape=jax.ShapeDtypeStruct((out_rows, LANES), jnp.float32),
         compiler_params=pltpu.CompilerParams(vmem_limit_bytes=VMEM_LIMIT),
@@ -143,7 +135,7 @@
             transcendentals=0,
         ),
         name="product",
-    )(left[0], left[1], right[0], right[1])
+    )(left, right)
 
 
 def gate_kernel(band_ref, gate_ref, out_ref):
@@ -155,7 +147,7 @@
 
 def gates_of(band, tri_gate):
     tok_dev, width, c = band.shape
-    rows = 4
+    rows = tok_dev // 4
     spec = pl.BlockSpec((rows, width, c), lambda i: (i, 0, 0))
     return pl.pallas_call(
         gate_kernel,
@@ -171,11 +163,10 @@
     )(band, tri_gate)
 
 
-def tail_kernel(rows, tok_dev, ch, own_ref, m1_ref, m2_ref, d_ref, band_ref, gate_ref, out_w_ref,
+def tail_kernel(rows, tok_dev, ch, o1_ref, o2_ref, m1_ref, m2_ref, d_ref, band_ref, gate_ref, out_w_ref,
                 proj_ref, band_out_ref, table_ref):
     step = pl.program_id(0)
     quarter = ch // 4
-    part = tok_dev // 2
     cp = proj_ref.shape[0]
     width, c = band_ref.shape[1:]
 
@@ -186,10 +177,13 @@
     places, updates = [], []
     for r in range(rows):
         row = step * rows + r
-        row = row + jnp.where(row >= part, PART_SLOT - part, 0)
         places.append(row)
         near = pl.ds(row, quarter, stride=SLOT)
-        packed = [own_ref[near, :], m1_ref[near, :] + m2_ref[near, :], d_ref[near, :]]
+        packed = [
+            o1_ref[near, :] + o2_ref[near, :],
+            m1_ref[near, :] + m2_ref[near, :],
+            d_ref[near, :].astype(jnp.float32),
+        ]
         prod = jnp.concatenate(
             [
                 jnp.concatenate([p[:, q * SLOT : (q + 1) * SLOT] for p in packed], axis=1)
@@ -204,14 +198,13 @@
     new = (band + gate * jnp.concatenate(updates, axis=0)).astype(jnp.bfloat16)
     zt = normalize(new).astype(jnp.bfloat16)
     lane = lax.broadcasted_iota(jnp.int32, (cp, width), 1)
-    used = lax.rem(lane, PART_SLOT) < part
+    used = lax.rem(lane, SLOT) < tok_dev
     plain = new.astype(jnp.float32)
     for r in range(rows):
         pieces = []
         for slot in (1, 0, 2):
-            for half in range(2):
-                at = r * width + slot * SLOT + half * PART_SLOT
-                pieces.append(plain[at : at + part])
+            at = r * width + slot * SLOT
+            pieces.append(plain[at : at + tok_dev])
         band_out_ref[r] = jnp.concatenate(pieces, axis=0).astype(jnp.bfloat16)
         tok = dot(proj_ref[...], zt[r * width : (r + 1) * width], NT)
         tok = jnp.where(used, tok, 0.0)
@@ -219,7 +212,7 @@
         table_ref[pl.ds(places[r], cp, stride=SLOT), :] = tok
 
 
-def tail(own, m1, m2, d, band, gate, tri_out, proj_t):
+def tail(o1, o2, m1, m2, d, band, gate, tri_out, proj_t):
     tok_dev, width, c = band.shape
     ch = tri_out.shape[0]
     cp = proj_t.shape[0]
@@ -229,7 +222,7 @@
     return pl.pallas_call(
         functools.partial(tail_kernel, rows, tok_dev, ch),
         grid=(tok_dev // rows,),
-        in_specs=[whole(own), whole(m1), whole(m2), whole(d), band_spec, band_spec,
+        in_specs=[whole(o1), whole(o2), whole(m1), whole(m2), whole(d), band_spec, band_spec,
                   whole(tri_out), whole(proj_t)],
         out_specs=[
             pl.BlockSpec((rows, 3 * tok_dev, c), lambda i: (i, 0, 0)),
@@ -241,15 +234,14 @@
         ],
         compiler_params=pltpu.CompilerParams(vmem_limit_bytes=VMEM_LIMIT),
         name="tail",
-    )(own, m1, m2, d, band, gate, tri_out, proj_t)
-
-
-def atom_kernel(devices, heads, blocks, mix_ref, table_ref, qtok_ref, ktok_ref, valid_ref,
-                offset_ref, cq_ref, ck_ref, act_ref, cond_ref, w_ref, out_ref,
+    )(o1, o2, m1, m2, d, band, gate, tri_out, proj_t)
+
+
+def atom_kernel(devices, heads, blocks, tok_dev, mix_ref, table_ref, q_ref, k_ref, act_ref, cond_ref, w_ref, out_ref,
                 ext, bias, planes, send_sem, recv_sem):
     atoms, width = act_ref.shape
     span = atoms + 2 * HALO
-    cp = ck_ref.shape[0]
+    cp = k_ref.shape[0] - 2
     head_dim = width // heads
     me = lax.axis_index("tok") * 2 + lax.axis_index("atm")
     above, below = me + 1, me - 1
@@ -343,18 +335,26 @@
 
     normed = begin(0, state)
 
-    qhot = (qtok_ref[...] == lax.broadcasted_iota(jnp.int32, (atoms, SLOT), 1)).astype(jnp.float32)
+    shard = lax.axis_index("tok")
+    qtok = q_ref[:, cp : cp + 1].astype(jnp.int32) - shard * tok_dev
+    ktok = k_ref[cp : cp + 1, :].astype(jnp.int32) - (shard - 1) * tok_dev
+    ktok = jnp.where(
+        ktok < tok_dev,
+        ktok + SLOT,
+        jnp.where(ktok < 2 * tok_dev, ktok - tok_dev, ktok + 2 * (SLOT - tok_dev)),
+    )
+    qhot = (qtok == lax.broadcasted_iota(jnp.int32, (atoms, SLOT), 1)).astype(jnp.float32)
     qhot = qhot.astype(jnp.bfloat16)
-    khot = (ktok_ref[...] == lax.broadcasted_iota(jnp.int32, (LANES, span), 0)).astype(jnp.float32)
+    khot = (ktok == lax.broadcasted_iota(jnp.int32, (LANES, span), 0)).astype(jnp.float32)
     khot = khot.astype(jnp.bfloat16)
     picked = dot(table_ref[...].astype(jnp.bfloat16), khot).astype(jnp.bfloat16)
     for c in range(cp):
         sel = dot(qhot, picked[c * SLOT : (c + 1) * SLOT])
-        planes[c] = sel + cq_ref[:, c : c + 1] + ck_ref[c : c + 1, :]
+        planes[c] = sel + q_ref[:, c : c + 1] + k_ref[c : c + 1, :]
     key = lax.broadcasted_iota(jnp.int32, (atoms, span), 1)
-    begin_key = offset_ref[...]
+    begin_key = q_ref[:, cp + 1 : cp + 2].astype(jnp.int32)
     live = jnp.logical_and(key >= begin_key, key < begin_key + KW)
-    live = jnp.logical_and(live, valid_ref[...] > 0)
+    live = jnp.logical_and(live, k_ref[cp + 1 : cp + 2, :] > 0.5)
     outs = blocks * heads
     rows = 16
 
@@ -395,20 +395,20 @@
     out_ref[...] = state.astype(jnp.bfloat16)
 
 
-def atoms_part(mix, table, qtok, ktok, valid, offset, cq, ck, act, cond, weights, devices, heads):
+def atoms_part(mix, table, q, k, act, cond, weights, devices, heads, tok_dev):
     atoms, width = act.shape
     span = atoms + 2 * HALO
     blocks = weights.shape[0]
     vmem = pl.BlockSpec(memory_space=pltpu.VMEM)
     return pl.pallas_call(
-        functools.partial(atom_kernel, devices, heads, blocks),
-        in_specs=[pl.BlockSpec(memory_space=pltpu.SMEM)] + [vmem] * 10,
+        functools.partial(atom_kernel, devices, heads, blocks, tok_dev),
+        in_specs=[pl.BlockSpec(memory_space=pltpu.SMEM)] + [vmem] * 6,
         out_specs=vmem,
         out_shape=jax.ShapeDtypeStruct(act.shape, jnp.bfloat16),
         scratch_shapes=[
             pltpu.VMEM((blocks, span, width), jnp.bfloat16),
             pltpu.VMEM((blocks * heads, atoms, span), jnp.float32),
-            pltpu.VMEM((ck.shape[0], atoms, span), jnp.float32),
+            pltpu.VMEM((k.shape[0] - 2, atoms, span), jnp.float32),
             pltpu.SemaphoreType.DMA((blocks, 2)),
             pltpu.SemaphoreType.DMA((blocks, 2)),
         ],
@@ -416,7 +416,7 @@
             collective_id=0, has_side_effects=True, vmem_limit_bytes=VMEM_LIMIT
         ),
         name="atoms",
-    )(mix, table, qtok, ktok, valid, offset, cq, ck, act, cond, weights)
+    )(mix, table, q, k, act, cond, weights)
 
 
 def local(
@@ -445,86 +445,62 @@
     down = [(i + 1, i) for i in range(groups - 1)]
 
     half = tokens // 2
-    part = tok_dev // 2
     chunk = 8 * tok_dev
+    swap = [(0, 1), (1, 0)]
     own = lax.dynamic_slice_in_dim(pair, core * half, half, 1)
-    low0 = lax.ppermute(own[:part], "tok", up)
-    low1 = lax.ppermute(own[part:], "tok", up)
+    low = lax.ppermute(own, "tok", up)
     w = jnp.swapaxes(tri_in, 1, 2).reshape(4 * ch, -1)
-    own0, own1 = project(own[:part], w, chunk), project(own[part:], w, chunk)
-    own_left, own_right = (own0[0], own1[0]), (own0[1], own1[1])
+    own_left, own_right = project(own, w, chunk)
     own_prod = product(own_left, own_right, ch)
-    own_prod = own_prod + lax.ppermute(own_prod, "atm", [(0, 1), (1, 0)])
+    own_other = lax.ppermute(own_prod, "atm", swap)
 
     padded = jnp.pad(pair, ((0, 0), (tok_dev, tok_dev), (0, 0)))
     band = lax.dynamic_slice_in_dim(padded, shard * tok_dev, 3 * tok_dev, 1)
-    band = band.reshape(tok_dev, 3, 2, part, -1)
+    band = band.reshape(tok_dev, 3, tok_dev, -1)
     band = jnp.concatenate([band[:, 1:2], band[:, 0:1], band[:, 2:3]], axis=1)
-    band = jnp.pad(band, ((0, 0), (0, 0), (0, 0), (0, PART_SLOT - part), (0, 0)))
+    band = jnp.pad(band, ((0, 0), (0, 0), (0, SLOT - tok_dev), (0, 0)))
     band = band.reshape(tok_dev, 3 * SLOT, -1)
     gate = gates_of(band, tri_gate)
 
     atoms = atom_act.shape[0]
     heads = bias_proj.shape[2]
     device = shard * lax.axis_size("atm") + core
-    labels = jnp.stack([atom_token, atom_mask], 1)
-    labels_ext = with_halo(labels, ((("tok", "atm"), 0),), HALO)
+    labels = jnp.stack([atom_token, atom_mask], 1).astype(jnp.float32)
     relu_cond = jax.nn.relu(atom_cond)
     query_term = jnp.dot(relu_cond, cond_pair[0], preferred_element_type=jnp.float32)
     key_term = jnp.dot(relu_cond, cond_pair[1], preferred_element_type=jnp.float32)
-    key_term_ext = with_halo(key_term, ((("tok", "atm"), 0),), HALO)
+    keys = jnp.concatenate([key_term, labels], 1)
+    keys = with_halo(keys, ((("tok", "atm"), 0),), HALO).T
     offsets = key_start - device * atoms + HALO
     projections = jnp.swapaxes(bias_proj, 0, 1).reshape(bias_proj.shape[1], -1).astype(jnp.float32)
     mixed = jnp.dot(
         pair_mlp.astype(jnp.float32), projections, precision=lax.Precision.HIGHEST
     )
-    spread = PART_SLOT - part
-    qtok = atom_token - shard * tok_dev
-    qtok = qtok + jnp.where(qtok >= part, spread, 0)
-    ktok = labels_ext[:, 0] - (shard - 1) * tok_dev
-    kgroup = (ktok >= tok_dev).astype(jnp.int32) + (ktok >= 2 * tok_dev).astype(jnp.int32)
-    ktok = ktok - kgroup * tok_dev
-    ktok = ktok + jnp.where(ktok >= part, spread, 0)
-    ktok = ktok + SLOT * jnp.where(kgroup == 0, 1, jnp.where(kgroup == 1, 0, 2))
-    early = (
-        jnp.concatenate([projections, mixed], 0),
-        qtok[:, None],
-        ktok[None, :],
-        labels_ext[:, 1][None, :],
-        jnp.repeat(offsets, QUERY_ATOMS)[:, None],
-        query_term,
-        key_term_ext.T,
-        band,
-        gate,
-        own_prod,
-        pair_proj.T,
-    )
-    low1, early = lax.optimization_barrier((low1, early))
-    mix, qtok, ktok, valid, offset, cq, ck, band, gate, own_prod, proj_t = early
-
-    low0, low1 = project(low0, w, chunk), project(low1, w, chunk)
-    low_left, low_right = (low0[0], low1[0]), (low0[1], low1[1])
-    swap = [(0, 1), (1, 0)]
+    starts = jnp.repeat(offsets, QUERY_ATOMS).astype(jnp.float32)
+    queries = jnp.concatenate([query_term, labels[:, :1], starts[:, None]], 1)
+    mix = jnp.concatenate([projections, mixed], 0)
+    early = (mix, queries, keys, band, gate, own_prod, own_other, pair_proj.T)
+    low, early = lax.optimization_barrier((low, early))
+    mix, queries, keys, band, gate, own_prod, own_other, proj_t = early
+
+    low_left, low_right = project(low, w, chunk)
     back = product(low_left, own_right, ch)
     back = (back + lax.ppermute(back, "atm", swap)).astype(jnp.bfloat16)
     main = product(own_left, low_right, ch)
     other = lax.ppermute(main, "atm", swap)
     back = lax.ppermute(back, "tok", down).astype(jnp.float32)
-    pair_band, table = tail(own_prod, main, other, back, band, gate, tri_out, proj_t)
+    pair_band, table = tail(own_prod, own_other, main, other, back, band, gate, tri_out, proj_t)
     atoms_out = atoms_part(
         mix,
         table,
-        qtok,
-        ktok,
-        valid,
-        offset,
-        cq,
-        ck,
+        queries,
+        keys,
         atom_act,
         atom_cond,
         block_weights,
         groups * lax.axis_size("atm"),
         heads,
+        tok_dev,
     )
     return (pair_band, atoms_out)
 

time: 125 us -> 111 us (0.89)
  starting transfers between devices: 22.1 us -> 14.4 us
  waiting for transfers between devices: 11.2 us -> 6.47 us
  Pallas kernels: 71.9 us -> 75.5 us
  other arithmetic: 5.78 us -> 3.28 us
  local copies, waits for them, and re-layouts: 11.3 us -> 9.07 us
    ppermute x2 -> x1, starting transfers between devices: 8.43 us -> 3.03 us  [with_halo(): before = lax.ppermute(last, axis, up)]
    ppermute x2 -> x1, waiting for transfers between devices: 3.71 us -> 0.01 us  [with_halo(): after = lax.ppermute(leading, axis, down)]
    pallas_call x4 -> x2, Pallas kernels: 23.3 us -> 26.9 us  [project(): pl.pallas_call(functools.partial(project_kernel, rows, chunk, tiles), gri...]
    ppermute x3 -> x2, starting transfers between devices: 7.47 us -> 4.06 us  [the longest x1 3.11 us: local(): low = lax.ppermute(own, 'tok', up)]
    slice x3 -> x1, local copies, waits for them, and re-layouts: 2.85 us -> 0.01 us  [local(): queries = jnp.concatenate([query_term, labels[:, :1], starts[:, None]], 1)]
    dynamic_slice x0 -> x1, local copies, waits for them, and re-layouts: none -> 2.76 us  [local(): own = lax.dynamic_slice_in_dim(pair, core * half, half, 1)]
    add x3 -> x0, other arithmetic: 2.45 us -> none  [the longest x1 1.92 us: local(): own_prod = own_prod + lax.ppermute(own_prod, 'atm', [(0, 1), (1, 0)])]
    ppermute x1, starting transfers between devices: 1.92 us -> 3.86 us  [local(): back = lax.ppermute(back, 'tok', down).astype(jnp.float32)]
  transfers between devices with their start and end apart: 10 -> 7, of which waited for: 2 -> 1; matrix products, arithmetic and copies ran while one was open for 10% -> 7% of each run, Pallas kernels for 28% -> 26%
where the time goes in v3:
time: 111 us; the launch traced here: 110 us
  Pallas kernels  75.5 us (68%)
  starting transfers between devices  14.4 us (13%)
  local copies, waits for them, and re-layouts  9.07 us (8%)
  waiting for transfers between devices  6.47 us (6%)
  other arithmetic  3.28 us (3%)
    pallas_call x2, Pallas kernels, project(): pl.pallas_call(functools.partial(project_kernel, rows, chunk, tiles), gri...  26.9 us
    pallas_call x1, Pallas kernels, atoms_part(): pl.pallas_call(functools.partial(atom_kernel, devices, heads, blocks, tok...  19.4 us
    pallas_call x3, Pallas kernels, product(): pl.pallas_call(functools.partial(product_kernel, ch), grid=(chunks,), in_...  16.1 us
    pallas_call x1, Pallas kernels, tail(): pl.pallas_call(functools.partial(tail_kernel, rows, tok_dev, ch), grid=(t...  9.07 us
    ppermute x1, waiting for transfers between devices, local(): back = lax.ppermute(back, 'tok', down).astype(jnp.float32)  6.46 us
    pallas_call x1, Pallas kernels, gates_of(): pl.pallas_call(gate_kernel, grid=(tok_dev // rows,), in_specs=[spec, pl.B...  4.1 us
    ppermute x1, starting transfers between devices, local(): back = lax.ppermute(back, 'tok', down).astype(jnp.float32)  3.86 us
    ppermute x1, starting transfers between devices, local(): low = lax.ppermute(own, 'tok', up)  3.11 us
  transfers between devices with their start and end apart: 7, of which 1 were waited for; matrix products, arithmetic and copies ran while one was open for 7% of the time, Pallas kernels for 26%

profile of v3, /device:TPU:23, one launch (start us, length us, event | category | flops | bytes accessed | tf_op | source)
XLA Modules:
  0.0 110.0 jit_solution(32495305531680981)
XLA Ops:
  0.6 0.0 copy-start
  0.7 2.8 %constant_dynamic-slice_fusion.x_ref = bf16[28,224,128]{2,1,0:T(8,128)(2,1)} fusion(bf16[28,448,128]{2,1,0:T(8,128)(2,1)} %param.15, s32[]{:T(128)S(6)} %select_n.6), kind=kLoop, calls=%fused_computation.25 | loop fusion | bytes 3211268 | tf_op jit(solution)/shard_map/dynamic_slice | solution.py:450
  3.4 3.1 %collective-permute-start = (bf16[28,224,128]{2,1,0:T(8,128)(2,1)}, bf16[28,224,128]{2,1,0:T(8,128)(2,1)}, u32[]{:S(2)}, u32[]{:S(2)}) collective-permute-start(bf16[28,224,128]{2,1,0:T(8,128)(2,1)} %constant_dynamic-slice_fusion.x_ref), channel_id=1, source_target_pairs={{0,2},{2,4},{4,6},{6,8},{8,10},{10,12},{12,14},{14,16},{16,18},{18... | collective-permute-start | bytes 4816904 | tf_op jit(solution)/shard_map/ppermute | solution.py:451
  6.5 0.8 copy.30
  7.3 13.4 %project.2 = (bf16[1,2,4096,128]{3,2,1,0:T(8,128)(2,1)}, bf16[1,2,4096,128]{3,2,1,0:T(8,128)(2,1)}) custom-call(bf16[28,224,128]{2,1,0:T(8,128)(2,1)} %constant_dynamic-slice_fusion.x_ref, bf16[512,128]{1,0:T(8,128)(2,1)} %bitcast.22), custom_call_target="tpu_custom_call" | custom-call | flops 822083584 | bytes 12845056 | tf_op jit(solution)/shard_map/project/pallas_call | solution.py:81
  20.7 0.0 copy-start.6
  20.7 0.0 copy-start.10
  20.8 0.0 copy-start.7
  20.8 0.0 copy-start.1
  20.8 5.5 %product.3.o1_ref = f32[1024,128]{1,0:T(8,128)} custom-call(bf16[1,2,4096,128]{3,2,1,0:T(8,128)(2,1)} %get-tuple-element.17.a_ref, bf16[1,2,4096,128]{3,2,1,0:T(8,128)(2,1)} %get-tuple-element.18.b_ref), custom_call_target="tpu_custom_call" | custom-call | flops 67108864 | bytes 16777216 | tf_op jit(solution)/shard_map/product/pallas_call | solution.py:125
  26.2 1.0 collective-permute-start.3
  27.2 0.0 copy-done.9
  27.2 0.1 fusion.5
  27.4 0.1 slice_maximum_fusion
  27.4 3.0 %collective-permute-start.1 = (f32[64,18]{0,1:T(8,128)S(1)}, f32[64,18]{0,1:T(8,128)S(1)}, u32[]{:S(2)}, u32[]{:S(2)}) collective-permute-start(f32[64,18]{0,1:T(8,128)S(1)} %get-tuple-element.35), channel_id=1, source_target_pairs={{0,1},{1,2},{2,3},{3,4},{4,5},{5,6},{6,7},{7,8},{8,9},{9,10},{10,1... | collective-permute-start | bytes 13832 | tf_op jit(solution)/shard_map/ppermute | solution.py:28
  30.5 1.9 %collective-permute-start.2 = (f32[64,18]{0,1:T(8,128)S(1)}, f32[64,18]{0,1:T(8,128)S(1)}, u32[]{:S(2)}, u32[]{:S(2)}) collective-permute-start(f32[64,18]{0,1:T(8,128)S(1)} %get-tuple-element.36), channel_id=1, source_target_pairs={{1,0},{2,1},{3,2},{4,3},{5,4},{6,5},{7,6},{8,7},{9,8},{10,9},{11,1... | collective-permute-start | bytes 13832 | tf_op jit(solution)/shard_map/ppermute | solution.py:29
  32.4 0.1 broadcast_in_dim.4
  32.5 0.1 convert_element_type.34
  32.6 0.1 copy.28
  32.7 0.1 fusion.18
  32.8 0.6 pad_maximum_fusion.mix_ref
  33.5 1.0 pad_dynamic-slice_fusion
  34.5 0.1 fusion.7
  34.7 1.2 %reshape.29 = bf16[28,3,28,128]{3,2,1,0:T(8,128)(2,1)S(1)} reshape(bf16[28,84,128]{2,1,0:T(8,128)(2,1)} %pad_dynamic-slice_fusion) | data formatting | bytes 1204224 | tf_op jit(solution)/shard_map/reshape | solution.py:459
  35.9 0.1 fusion.17
  35.9 1.0 fusion.4
  36.9 4.1 %gate.1.gate_ref = f32[28,96,128]{2,1,0:T(8,128)} custom-call(bf16[28,96,128]{2,1,0:T(8,128)(2,1)} %bitcast.19, bf16[128,128]{1,0:T(8,128)(2,1)} %gate_ref.1), custom_call_target="tpu_custom_call" | custom-call | flops 88080384 | bytes 5505024 | tf_op jit(solution)/shard_map/gate/pallas_call | solution.py:152
  41.0 0.0 collective-permute-done.1
  41.0 0.0 collective-permute-done.2
  41.0 0.7 maximum_bitcast_fusion.k_ref
  41.7 0.0 collective-permute-done.3.o2_ref
  41.7 0.0 collective-permute-done.x_ref
  41.7 13.5 %project.3 = (bf16[1,2,4096,128]{3,2,1,0:T(8,128)(2,1)}, bf16[1,2,4096,128]{3,2,1,0:T(8,128)(2,1)}) custom-call(bf16[28,224,128]{2,1,0:T(8,128)(2,1)} %collective-permute-done.x_ref, bf16[512,128]{1,0:T(8,128)(2,1)} %bitcast.23), custom_call_target="tpu_custom_call" | custom-call | flops 822083584 | bytes 12845056 | tf_op jit(solution)/shard_map/project/pallas_call | solution.py:81
  55.2 5.3 %product.5 = f32[1024,128]{1,0:T(8,128)} custom-call(bf16[1,2,4096,128]{3,2,1,0:T(8,128)(2,1)} %get-tuple-element.23.a_ref, bf16[1,2,4096,128]{3,2,1,0:T(8,128)(2,1)} %get-tuple-element.18.b_ref), custom_call_target="tpu_custom_call" | custom-call | flops 67108864 | bytes 16777216 | tf_op jit(solution)/shard_map/product/pallas_call | solution.py:125
  60.4 1.6 %collective-permute-start.5 = (f32[1024,128]{1,0:T(8,128)}, f32[1024,128]{1,0:T(8,128)S(1)}, u32[]{:S(2)}, u32[]{:S(2)}) collective-permute-start(f32[1024,128]{1,0:T(8,128)} %product.5), channel_id=1, source_target_pairs={{0,1},{1,0},{2,3},{3,2},{4,5},{5,4},{6,7},{7,6},{8,9},{9,8},{10,11... | collective-permute-start | bytes 1572872 | tf_op jit(solution)/shard_map/ppermute | solution.py:488
  62.0 5.3 %product.4.m1_ref = f32[1024,128]{1,0:T(8,128)} custom-call(bf16[1,2,4096,128]{3,2,1,0:T(8,128)(2,1)} %get-tuple-element.17.a_ref, bf16[1,2,4096,128]{3,2,1,0:T(8,128)(2,1)} %get-tuple-element.22.b_ref), custom_call_target="tpu_custom_call" | custom-call | flops 67108864 | bytes 16777216 | tf_op jit(solution)/shard_map/product/pallas_call | solution.py:125
  67.3 0.0 collective-permute-start.4
  67.3 0.0 collective-permute-done.5
  67.3 0.1 add_convert_fusion
  67.4 3.9 %collective-permute-start.6 = (bf16[1024,128]{1,0:T(8,128)(2,1)S(1)}, bf16[1024,128]{1,0:T(8,128)(2,1)S(1)}, u32[]{:S(2)}, u32[]{:S(2)}) collective-permute-start(bf16[1024,128]{1,0:T(8,128)(2,1)S(1)} %add_convert_fusion), channel_id=1, source_target_pairs={{2,0},{4,2},{6,4},{8,6},{10,8},{12,10},{14,12},{16,14},{18,16},{20... | collective-permute-start | bytes 786440 | tf_op jit(solution)/shard_map/ppermute | solution.py:491
  71.3 0.7 copy.31.q_ref
  72.0 6.5 %collective-permute-done.6 = bf16[1024,128]{1,0:T(8,128)(2,1)S(1)} collective-permute-done((bf16[1024,128]{1,0:T(8,128)(2,1)S(1)}, bf16[1024,128]{1,0:T(8,128)(2,1)S(1)}, u32[]{:S(2)}, u32[]{:S(2)}) %collective-permute-start.6) | collective-permute-done | bytes 262176 | tf_op jit(solution)/shard_map/ppermute | solution.py:491
  78.5 0.8 convert_element_type.36.d_ref
  79.3 0.0 collective-permute-done.4.m2_ref
  79.3 0.8 copy-done.3
  80.1 9.1 %tail.1 = (bf16[28,84,128]{2,1,0:T(8,128)(2,1)}, f32[512,128]{1,0:T(8,128)}) custom-call(f32[1024,128]{1,0:T(8,128)} %product.3.o1_ref, f32[1024,128]{1,0:T(8,128)} %collective-permute-done.3.o2_ref, f32[1024,128]{1,0:T(8,128)} %product.4.m1_ref, f32[1024,128]{1,0:T(8,128)} %copy-done.3, f32[1024,128]{1,0:T(8,128)} %convert_element_type.36.d_ref, ...), custom_call_target="tpu_custom_call" | custom-call | tf_op jit(solution)/shard_map/tail/pallas_call | solution.py:222
  89.2 19.4 %atoms.1 = bf16[128,128]{1,0:T(8,128)(2,1)} custom-call(f32[32,12]{1,0:T(8,128)} %pad_maximum_fusion.mix_ref, f32[512,128]{1,0:T(8,128)} %get-tuple-element.29.table_ref, f32[128,18]{1,0:T(8,128)} %copy.31.q_ref, f32[18,256]{1,0:T(8,128)} %maximum_bitcast_fusion.k_ref, bf16[128,128]{1,0:T(8,128)(2,1)} %act_ref.1, bf16[128,128]{1,0:T(8,128)(2,1)} %cond_ref.1, ...), custom_call_target="tpu_custom_call" | custom-call | tf_op jit(solution)/shard_map/atoms/pallas_call | solution.py:403
  108.6 1.4 %copy.34 = bf16[128,128]{1,0:T(8,128)(2,1)} copy(bf16[128,128]{1,0:T(8,128)(2,1)} %atoms.1) | data formatting | bytes 65536
  (21 shorter events, 0.1 us)
Async XLA Ops:
  0.6 32.1 %copy-start = (bf16[16,16]{1,0:T(8,128)(2,1)S(1)}, bf16[16,16]{1,0:T(8,128)(2,1)}, u32[]{:S(2)}) copy-start(bf16[16,16]{1,0:T(8,128)(2,1)} %param.23) | copy-start | bytes 1540
  0.7 5.9 %copy-start.5 = (bf16[4,128,128]{2,1,0:T(8,128)(2,1)S(1)}, bf16[4,128,128]{2,1,0:T(8,128)(2,1)}, u32[]{:S(2)}) copy-start(bf16[4,128,128]{2,1,0:T(8,128)(2,1)} %param.16) | copy-start | bytes 393220
  3.4 38.3 %collective-permute-start = (bf16[28,224,128]{2,1,0:T(8,128)(2,1)}, bf16[28,224,128]{2,1,0:T(8,128)(2,1)}, u32[]{:S(2)}, u32[]{:S(2)}) collective-permute-start(bf16[28,224,128]{2,1,0:T(8,128)(2,1)} %constant_dynamic-slice_fusion.x_ref), channel_id=1, source_target_pairs={{0,2},{2,4},{4,6},{6,8},{8,10},{10,12},{12,14},{14,16},{16,18},{18... | collective-permute-start | bytes 4816904 | tf_op jit(solution)/shard_map/ppermute | solution.py:451
  20.7 6.5 %copy-start.8 = (s32[128]{0:T(128)S(1)}, s32[128]{0:T(128)}, u32[]{:S(2)}) copy-start(s32[128]{0:T(128)} %param.27) | copy-start | bytes 1540
  20.7 6.5 %copy-start.9 = (s32[128]{0:T(128)S(1)}, s32[128]{0:T(128)}, u32[]{:S(2)}) copy-start(s32[128]{0:T(128)} %param.26) | copy-start | bytes 1540
  20.7 6.5 %copy-start.4 = (bf16[128,128]{1,0:T(8,128)(2,1)S(1)}, bf16[128,128]{1,0:T(8,128)(2,1)}, u32[]{:S(2)}) copy-start(bf16[128,128]{1,0:T(8,128)(2,1)} %cond_ref.1) | copy-start | bytes 98308
  20.7 6.5 %copy-start.6 = (bf16[2,128,16]{1,2,0:T(8,128)(2,1)S(1)}, bf16[2,128,16]{1,2,0:T(8,128)(2,1)}, u32[]{:S(2)}) copy-start(bf16[2,128,16]{1,2,0:T(8,128)(2,1)} %param.22) | copy-start | bytes 24580
  20.7 11.7 %copy-start.10 = (s32[4]{0:T(128)S(1)}, s32[4]{0:T(128)}, u32[]{:S(2)}) copy-start(s32[4]{0:T(128)} %param.28) | copy-start | bytes 52
  20.8 11.8 %copy-start.7 = (bf16[3,16,4]{1,2,0:T(4,128)(2,1)S(1)}, bf16[3,16,4]{1,2,0:T(4,128)(2,1)}, u32[]{:S(2)}) copy-start(bf16[3,16,4]{1,2,0:T(4,128)(2,1)} %param.24) | copy-start | bytes 1156
  20.8 12.7 %copy-start.1 = (bf16[28,448,128]{2,1,0:T(8,128)(2,1)S(1)}, bf16[28,448,128]{2,1,0:T(8,128)(2,1)}, u32[]{:S(2)}) copy-start(bf16[28,448,128]{2,1,0:T(8,128)(2,1)} %param.15) | copy-start | bytes 9633796
  26.2 15.5 %collective-permute-start.3 = (f32[1024,128]{1,0:T(8,128)}, f32[1024,128]{1,0:T(8,128)}, u32[]{:S(2)}, u32[]{:S(2)}) collective-permute-start(f32[1024,128]{1,0:T(8,128)} %product.3.o1_ref), channel_id=1, source_target_pairs={{0,1},{1,0},{2,3},{3,2},{4,5},{5,4},{6,7},{7,6},{8,9},{9,8},{10,11... | collective-permute-start | bytes 1572872 | tf_op jit(solution)/shard_map/ppermute | solution.py:455
  27.4 13.6 %collective-permute-start.1 = (f32[64,18]{0,1:T(8,128)S(1)}, f32[64,18]{0,1:T(8,128)S(1)}, u32[]{:S(2)}, u32[]{:S(2)}) collective-permute-start(f32[64,18]{0,1:T(8,128)S(1)} %get-tuple-element.35), channel_id=1, source_target_pairs={{0,1},{1,2},{2,3},{3,4},{4,5},{5,6},{6,7},{7,8},{8,9},{9,10},{10,1... | collective-permute-start | bytes 13832 | tf_op jit(solution)/shard_map/ppermute | solution.py:28
  30.5 10.5 %collective-permute-start.2 = (f32[64,18]{0,1:T(8,128)S(1)}, f32[64,18]{0,1:T(8,128)S(1)}, u32[]{:S(2)}, u32[]{:S(2)}) collective-permute-start(f32[64,18]{0,1:T(8,128)S(1)} %get-tuple-element.36), channel_id=1, source_target_pairs={{1,0},{2,1},{3,2},{4,3},{5,4},{6,5},{7,6},{8,7},{9,8},{10,9},{11,1... | collective-permute-start | bytes 13832 | tf_op jit(solution)/shard_map/ppermute | solution.py:29
  60.4 6.9 %collective-permute-start.5 = (f32[1024,128]{1,0:T(8,128)}, f32[1024,128]{1,0:T(8,128)S(1)}, u32[]{:S(2)}, u32[]{:S(2)}) collective-permute-start(f32[1024,128]{1,0:T(8,128)} %product.5), channel_id=1, source_target_pairs={{0,1},{1,0},{2,3},{3,2},{4,5},{5,4},{6,7},{7,6},{8,9},{9,8},{10,11... | collective-permute-start | bytes 1572872 | tf_op jit(solution)/shard_map/ppermute | solution.py:488
  62.0 5.3 %copy-start.2 = (f32[1024,128]{1,0:T(8,128)S(1)}, f32[1024,128]{1,0:T(8,128)}, u32[]{:S(2)}) copy-start(f32[1024,128]{1,0:T(8,128)} %product.5) | copy-start | bytes 1572868
  67.3 12.0 %collective-permute-start.4 = (f32[1024,128]{1,0:T(8,128)}, f32[1024,128]{1,0:T(8,128)S(1)}, u32[]{:S(2)}, u32[]{:S(2)}) collective-permute-start(f32[1024,128]{1,0:T(8,128)} %product.4.m1_ref), channel_id=1, source_target_pairs={{0,1},{1,0},{2,3},{3,2},{4,5},{5,4},{6,7},{7,6},{8,9},{9,8},{10,11... | collective-permute-start | bytes 1572872 | tf_op jit(solution)/shard_map/ppermute | solution.py:490
  67.4 11.1 %collective-permute-start.6 = (bf16[1024,128]{1,0:T(8,128)(2,1)S(1)}, bf16[1024,128]{1,0:T(8,128)(2,1)S(1)}, u32[]{:S(2)}, u32[]{:S(2)}) collective-permute-start(bf16[1024,128]{1,0:T(8,128)(2,1)S(1)} %add_convert_fusion), channel_id=1, source_target_pairs={{2,0},{4,2},{6,4},{8,6},{10,8},{12,10},{14,12},{16,14},{18,16},{20... | collective-permute-start | bytes 786440 | tf_op jit(solution)/shard_map/ppermute | solution.py:491
  79.3 0.8 copy-start.3

commit v4 on v3

--- a/solution.py
+++ b/solution.py
@@ -216,7 +216,7 @@
     tok_dev, width, c = band.shape
     ch = tri_out.shape[0]
     cp = proj_t.shape[0]
-    rows = 4
+    rows = tok_dev // 4
     whole = lambda x: pl.BlockSpec(x.shape, lambda i: (0, 0))
     band_spec = pl.BlockSpec((rows, width, c), lambda i: (i, 0, 0))
     return pl.pallas_call(
@@ -486,9 +486,11 @@
     low_left, low_right = project(low, w, chunk)
     back = product(low_left, own_right, ch)
     back = (back + lax.ppermute(back, "atm", swap)).astype(jnp.bfloat16)
+    own_left, back = lax.optimization_barrier((own_left, back))
+    back = lax.ppermute(back, "tok", down)
     main = product(own_left, low_right, ch)
     other = lax.ppermute(main, "atm", swap)
-    back = lax.ppermute(back, "tok", down).astype(jnp.float32)
+    back = back.astype(jnp.float32)
     pair_band, table = tail(own_prod, own_other, main, other, back, band, gate, tri_out, proj_t)
     atoms_out = atoms_part(
         mix,

time: 111 us -> 112 us (level)
  waiting for transfers between devices: 6.47 us -> 8.98 us
  Pallas kernels: 75.5 us -> 73.4 us
    ppermute x1, waiting for transfers between devices: 0.01 us -> 1.75 us  [local(): back = (back + lax.ppermute(back, 'atm', swap)).astype(jnp.bfloat16)]
    pallas_call x1, Pallas kernels: 9.07 us -> 7.45 us  [tail(): pl.pallas_call(functools.partial(tail_kernel, rows, tok_dev, ch), grid=(t...]
  transfers between devices with their start and end apart: 7 -> 7, of which waited for: 1 -> 2; matrix products, arithmetic and copies ran while one was open for 7% -> 7% of each run, Pallas kernels for 26% -> 21%
where the time goes in v4:
time: 112 us; the launch traced here: 111 us
  Pallas kernels  73.4 us (66%)
  starting transfers between devices  14.5 us (13%)
  local copies, waits for them, and re-layouts  9.05 us (8%)
  waiting for transfers between devices  8.98 us (8%)
  other arithmetic  4.34 us (4%)
    pallas_call x2, Pallas kernels, project(): pl.pallas_call(functools.partial(project_kernel, rows, chunk, tiles), gri...  26.9 us
    pallas_call x1, Pallas kernels, atoms_part(): pl.pallas_call(functools.partial(atom_kernel, devices, heads, blocks, tok...  19 us
    pallas_call x3, Pallas kernels, product(): pl.pallas_call(functools.partial(product_kernel, ch), grid=(chunks,), in_...  16 us
    pallas_call x1, Pallas kernels, tail(): pl.pallas_call(functools.partial(tail_kernel, rows, tok_dev, ch), grid=(t...  7.45 us
    ppermute x1, waiting for transfers between devices, local(): back = lax.ppermute(back, 'tok', down)  7.22 us
    pallas_call x1, Pallas kernels, gates_of(): pl.pallas_call(gate_kernel, grid=(tok_dev // rows,), in_specs=[spec, pl.B...  4.1 us
    ppermute x1, starting transfers between devices, local(): back = lax.ppermute(back, 'tok', down)  3.49 us
    ppermute x1, starting transfers between devices, local(): low = lax.ppermute(own, 'tok', up)  3.11 us
  transfers between devices with their start and end apart: 7, of which 2 were waited for; matrix products, arithmetic and copies ran while one was open for 7% of the time, Pallas kernels for 21%

profile of v4, /device:TPU:23, one launch (start us, length us, event | category | flops | bytes accessed | tf_op | source)
XLA Modules:
  0.0 111.5 jit_solution(12951659655285511392)
XLA Ops:
  0.6 0.0 copy-start
  0.7 2.8 %constant_dynamic-slice_fusion.x_ref = bf16[28,224,128]{2,1,0:T(8,128)(2,1)} fusion(bf16[28,448,128]{2,1,0:T(8,128)(2,1)} %param.15, s32[]{:T(128)S(6)} %select_n.6), kind=kLoop, calls=%fused_computation.25 | loop fusion | bytes 3211268 | tf_op jit(solution)/shard_map/dynamic_slice | solution.py:450
  3.4 3.1 %collective-permute-start = (bf16[28,224,128]{2,1,0:T(8,128)(2,1)}, bf16[28,224,128]{2,1,0:T(8,128)(2,1)}, u32[]{:S(2)}, u32[]{:S(2)}) collective-permute-start(bf16[28,224,128]{2,1,0:T(8,128)(2,1)} %constant_dynamic-slice_fusion.x_ref), channel_id=1, source_target_pairs={{0,2},{2,4},{4,6},{6,8},{8,10},{10,12},{12,14},{14,16},{16,18},{18... | collective-permute-start | bytes 4816904 | tf_op jit(solution)/shard_map/ppermute | solution.py:451
  6.5 0.8 copy.30
  7.3 13.4 %project.2 = (bf16[1,2,4096,128]{3,2,1,0:T(8,128)(2,1)}, bf16[1,2,4096,128]{3,2,1,0:T(8,128)(2,1)}) custom-call(bf16[28,224,128]{2,1,0:T(8,128)(2,1)} %constant_dynamic-slice_fusion.x_ref, bf16[512,128]{1,0:T(8,128)(2,1)} %bitcast.22), custom_call_target="tpu_custom_call" | custom-call | flops 822083584 | bytes 12845056 | tf_op jit(solution)/shard_map/project/pallas_call | solution.py:81
  20.7 0.0 copy-start.5
  20.7 0.0 copy-start.9
  20.7 0.0 copy-start.6
  20.7 0.0 copy-start.1
  20.8 5.4 %product.3.o1_ref = f32[1024,128]{1,0:T(8,128)} custom-call(bf16[1,2,4096,128]{3,2,1,0:T(8,128)(2,1)} %get-tuple-element.25.a_ref, bf16[1,2,4096,128]{3,2,1,0:T(8,128)(2,1)} %get-tuple-element.20.b_ref), custom_call_target="tpu_custom_call" | custom-call | flops 67108864 | bytes 16777216 | tf_op jit(solution)/shard_map/product/pallas_call | solution.py:125
  26.2 1.0 collective-permute-start.3
  27.2 0.0 copy-done.8
  27.2 0.1 fusion.5
  27.3 0.1 slice_maximum_fusion
  27.4 3.0 %collective-permute-start.1 = (f32[64,18]{0,1:T(8,128)S(1)}, f32[64,18]{0,1:T(8,128)S(1)}, u32[]{:S(2)}, u32[]{:S(2)}) collective-permute-start(f32[64,18]{0,1:T(8,128)S(1)} %get-tuple-element.39), channel_id=1, source_target_pairs={{0,1},{1,2},{2,3},{3,4},{4,5},{5,6},{6,7},{7,8},{8,9},{9,10},{10,1... | collective-permute-start | bytes 13832 | tf_op jit(solution)/shard_map/ppermute | solution.py:28
  30.4 1.9 %collective-permute-start.2 = (f32[64,18]{0,1:T(8,128)S(1)}, f32[64,18]{0,1:T(8,128)S(1)}, u32[]{:S(2)}, u32[]{:S(2)}) collective-permute-start(f32[64,18]{0,1:T(8,128)S(1)} %get-tuple-element.40), channel_id=1, source_target_pairs={{1,0},{2,1},{3,2},{4,3},{5,4},{6,5},{7,6},{8,7},{9,8},{10,9},{11,1... | collective-permute-start | bytes 13832 | tf_op jit(solution)/shard_map/ppermute | solution.py:29
  32.4 0.1 broadcast_in_dim.4
  32.5 0.1 convert_element_type.34
  32.6 0.1 copy.28
  32.7 0.1 fusion.18
  32.8 0.6 pad_maximum_fusion.mix_ref
  33.4 1.0 pad_dynamic-slice_fusion
  34.5 0.1 fusion.7
  34.6 1.2 %reshape.29 = bf16[28,3,28,128]{3,2,1,0:T(8,128)(2,1)S(1)} reshape(bf16[28,84,128]{2,1,0:T(8,128)(2,1)} %pad_dynamic-slice_fusion) | data formatting | bytes 1204224 | tf_op jit(solution)/shard_map/reshape | solution.py:459
  35.8 0.1 fusion.17
  35.9 1.0 fusion.4
  36.8 4.1 %gate.1.gate_ref = f32[28,96,128]{2,1,0:T(8,128)} custom-call(bf16[28,96,128]{2,1,0:T(8,128)(2,1)} %bitcast.19, bf16[128,128]{1,0:T(8,128)(2,1)} %gate_ref.1), custom_call_target="tpu_custom_call" | custom-call | flops 88080384 | bytes 5505024 | tf_op jit(solution)/shard_map/gate/pallas_call | solution.py:152
  40.9 0.0 collective-permute-done.1
  40.9 0.0 collective-permute-done.2
  41.0 0.7 maximum_bitcast_fusion.k_ref
  41.6 0.0 collective-permute-done.3.o2_ref
  41.6 0.0 collective-permute-done.x_ref
  41.6 13.5 %project.3 = (bf16[1,2,4096,128]{3,2,1,0:T(8,128)(2,1)}, bf16[1,2,4096,128]{3,2,1,0:T(8,128)(2,1)}) custom-call(bf16[28,224,128]{2,1,0:T(8,128)(2,1)} %collective-permute-done.x_ref, bf16[512,128]{1,0:T(8,128)(2,1)} %bitcast.23), custom_call_target="tpu_custom_call" | custom-call | flops 822083584 | bytes 12845056 | tf_op jit(solution)/shard_map/project/pallas_call | solution.py:81
  55.1 5.3 %product.4 = f32[1024,128]{1,0:T(8,128)} custom-call(bf16[1,2,4096,128]{3,2,1,0:T(8,128)(2,1)} %get-tuple-element.24.a_ref, bf16[1,2,4096,128]{3,2,1,0:T(8,128)(2,1)} %get-tuple-element.20.b_ref), custom_call_target="tpu_custom_call" | custom-call | flops 67108864 | bytes 16777216 | tf_op jit(solution)/shard_map/product/pallas_call | solution.py:125
  60.4 1.6 %collective-permute-start.4 = (f32[1024,128]{1,0:T(8,128)}, f32[1024,128]{1,0:T(8,128)S(1)}, u32[]{:S(2)}, u32[]{:S(2)}) collective-permute-start(f32[1024,128]{1,0:T(8,128)} %product.4), channel_id=1, source_target_pairs={{0,1},{1,0},{2,3},{3,2},{4,5},{5,4},{6,7},{7,6},{8,9},{9,8},{10,11... | collective-permute-start | bytes 1572872 | tf_op jit(solution)/shard_map/ppermute | solution.py:488
  62.0 1.7 %collective-permute-done.4 = f32[1024,128]{1,0:T(8,128)S(1)} collective-permute-done((f32[1024,128]{1,0:T(8,128)}, f32[1024,128]{1,0:T(8,128)S(1)}, u32[]{:S(2)}, u32[]{:S(2)}) %collective-permute-start.4) | collective-permute-done | bytes 524320 | tf_op jit(solution)/shard_map/ppermute | solution.py:488
  63.7 1.1 %add_convert_fusion = bf16[1024,128]{1,0:T(8,128)(2,1)S(1)} fusion(f32[1024,128]{1,0:T(8,128)} %product.4, f32[1024,128]{1,0:T(8,128)S(1)} %collective-permute-done.4), kind=kLoop, calls=%fused_computation.7 | loop fusion | flops 262144 | bytes 1310720 | tf_op jit(solution)/shard_map/convert_element_type | solution.py:488
  64.9 5.3 %product.5.m1_ref = f32[1024,128]{1,0:T(8,128)} custom-call(bf16[1,2,4096,128]{3,2,1,0:T(8,128)(2,1)} %get-tuple-element.25.a_ref, bf16[1,2,4096,128]{3,2,1,0:T(8,128)(2,1)} %get-tuple-element.26.b_ref), custom_call_target="tpu_custom_call" | custom-call | flops 67108864 | bytes 16777216 | tf_op jit(solution)/shard_map/product/pallas_call | solution.py:125
  70.2 0.4 collective-permute-start.5
  70.5 3.5 %collective-permute-start.6 = (bf16[1024,128]{1,0:T(8,128)(2,1)S(1)}, bf16[1024,128]{1,0:T(8,128)(2,1)S(1)}, u32[]{:S(2)}, u32[]{:S(2)}) collective-permute-start(bf16[1024,128]{1,0:T(8,128)(2,1)S(1)} %add_convert_fusion), channel_id=1, source_target_pairs={{2,0},{4,2},{6,4},{8,6},{10,8},{12,10},{14,12},{16,14},{18,16},{20... | collective-permute-start | bytes 786440 | tf_op jit(solution)/shard_map/ppermute | solution.py:490
  74.0 0.7 copy.31.q_ref
  74.8 7.2 %collective-permute-done.6 = bf16[1024,128]{1,0:T(8,128)(2,1)S(1)} collective-permute-done((bf16[1024,128]{1,0:T(8,128)(2,1)S(1)}, bf16[1024,128]{1,0:T(8,128)(2,1)S(1)}, u32[]{:S(2)}, u32[]{:S(2)}) %collective-permute-start.6) | collective-permute-done | bytes 262176 | tf_op jit(solution)/shard_map/ppermute | solution.py:490
  82.0 0.8 convert_element_type.36.d_ref
  82.8 0.0 collective-permute-done.5.m2_ref
  82.8 0.8 copy-done.2
  83.6 7.5 %tail.1 = (bf16[28,84,128]{2,1,0:T(8,128)(2,1)}, f32[512,128]{1,0:T(8,128)}) custom-call(f32[1024,128]{1,0:T(8,128)} %product.3.o1_ref, f32[1024,128]{1,0:T(8,128)} %collective-permute-done.3.o2_ref, f32[1024,128]{1,0:T(8,128)} %product.5.m1_ref, f32[1024,128]{1,0:T(8,128)} %copy-done.2, f32[1024,128]{1,0:T(8,128)} %convert_element_type.36.d_ref, ...), custom_call_target="tpu_custom_call" | custom-call | tf_op jit(solution)/shard_map/tail/pallas_call | solution.py:222
  91.1 19.0 %atoms.1 = bf16[128,128]{1,0:T(8,128)(2,1)} custom-call(f32[32,12]{1,0:T(8,128)} %pad_maximum_fusion.mix_ref, f32[512,128]{1,0:T(8,128)} %get-tuple-element.33.table_ref, f32[128,18]{1,0:T(8,128)} %copy.31.q_ref, f32[18,256]{1,0:T(8,128)} %maximum_bitcast_fusion.k_ref, bf16[128,128]{1,0:T(8,128)(2,1)} %act_ref.1, bf16[128,128]{1,0:T(8,128)(2,1)} %cond_ref.1, ...), custom_call_target="tpu_custom_call" | custom-call | tf_op jit(solution)/shard_map/atoms/pallas_call | solution.py:403
  110.1 1.4 %copy.34 = bf16[128,128]{1,0:T(8,128)(2,1)} copy(bf16[128,128]{1,0:T(8,128)(2,1)} %atoms.1) | data formatting | bytes 65536
  (19 shorter events, 0.1 us)
Async XLA Ops:
  0.6 32.1 %copy-start = (bf16[16,16]{1,0:T(8,128)(2,1)S(1)}, bf16[16,16]{1,0:T(8,128)(2,1)}, u32[]{:S(2)}) copy-start(bf16[16,16]{1,0:T(8,128)(2,1)} %param.23) | copy-start | bytes 1540
  0.7 5.9 %copy-start.4 = (bf16[4,128,128]{2,1,0:T(8,128)(2,1)S(1)}, bf16[4,128,128]{2,1,0:T(8,128)(2,1)}, u32[]{:S(2)}) copy-start(bf16[4,128,128]{2,1,0:T(8,128)(2,1)} %param.16) | copy-start | bytes 393220
  3.4 38.2 %collective-permute-start = (bf16[28,224,128]{2,1,0:T(8,128)(2,1)}, bf16[28,224,128]{2,1,0:T(8,128)(2,1)}, u32[]{:S(2)}, u32[]{:S(2)}) collective-permute-start(bf16[28,224,128]{2,1,0:T(8,128)(2,1)} %constant_dynamic-slice_fusion.x_ref), channel_id=1, source_target_pairs={{0,2},{2,4},{4,6},{6,8},{8,10},{10,12},{12,14},{14,16},{16,18},{18... | collective-permute-start | bytes 4816904 | tf_op jit(solution)/shard_map/ppermute | solution.py:451
  20.7 6.5 %copy-start.7 = (s32[128]{0:T(128)S(1)}, s32[128]{0:T(128)}, u32[]{:S(2)}) copy-start(s32[128]{0:T(128)} %param.27) | copy-start | bytes 1540
  20.7 6.5 %copy-start.8 = (s32[128]{0:T(128)S(1)}, s32[128]{0:T(128)}, u32[]{:S(2)}) copy-start(s32[128]{0:T(128)} %param.26) | copy-start | bytes 1540
  20.7 6.5 %copy-start.3 = (bf16[128,128]{1,0:T(8,128)(2,1)S(1)}, bf16[128,128]{1,0:T(8,128)(2,1)}, u32[]{:S(2)}) copy-start(bf16[128,128]{1,0:T(8,128)(2,1)} %cond_ref.1) | copy-start | bytes 98308
  20.7 6.5 %copy-start.5 = (bf16[2,128,16]{1,2,0:T(8,128)(2,1)S(1)}, bf16[2,128,16]{1,2,0:T(8,128)(2,1)}, u32[]{:S(2)}) copy-start(bf16[2,128,16]{1,2,0:T(8,128)(2,1)} %param.22) | copy-start | bytes 24580
  20.7 11.7 %copy-start.9 = (s32[4]{0:T(128)S(1)}, s32[4]{0:T(128)}, u32[]{:S(2)}) copy-start(s32[4]{0:T(128)} %param.28) | copy-start | bytes 52
  20.7 11.8 %copy-start.6 = (bf16[3,16,4]{1,2,0:T(4,128)(2,1)S(1)}, bf16[3,16,4]{1,2,0:T(4,128)(2,1)}, u32[]{:S(2)}) copy-start(bf16[3,16,4]{1,2,0:T(4,128)(2,1)} %param.24) | copy-start | bytes 1156
  20.7 12.7 %copy-start.1 = (bf16[28,448,128]{2,1,0:T(8,128)(2,1)S(1)}, bf16[28,448,128]{2,1,0:T(8,128)(2,1)}, u32[]{:S(2)}) copy-start(bf16[28,448,128]{2,1,0:T(8,128)(2,1)} %param.15) | copy-start | bytes 9633796
  26.2 15.4 %collective-permute-start.3 = (f32[1024,128]{1,0:T(8,128)}, f32[1024,128]{1,0:T(8,128)}, u32[]{:S(2)}, u32[]{:S(2)}) collective-permute-start(f32[1024,128]{1,0:T(8,128)} %product.3.o1_ref), channel_id=1, source_target_pairs={{0,1},{1,0},{2,3},{3,2},{4,5},{5,4},{6,7},{7,6},{8,9},{9,8},{10,11... | collective-permute-start | bytes 1572872 | tf_op jit(solution)/shard_map/ppermute | solution.py:455
  27.4 13.5 %collective-permute-start.1 = (f32[64,18]{0,1:T(8,128)S(1)}, f32[64,18]{0,1:T(8,128)S(1)}, u32[]{:S(2)}, u32[]{:S(2)}) collective-permute-start(f32[64,18]{0,1:T(8,128)S(1)} %get-tuple-element.39), channel_id=1, source_target_pairs={{0,1},{1,2},{2,3},{3,4},{4,5},{5,6},{6,7},{7,8},{8,9},{9,10},{10,1... | collective-permute-start | bytes 13832 | tf_op jit(solution)/shard_map/ppermute | solution.py:28
  30.4 10.5 %collective-permute-start.2 = (f32[64,18]{0,1:T(8,128)S(1)}, f32[64,18]{0,1:T(8,128)S(1)}, u32[]{:S(2)}, u32[]{:S(2)}) collective-permute-start(f32[64,18]{0,1:T(8,128)S(1)} %get-tuple-element.40), channel_id=1, source_target_pairs={{1,0},{2,1},{3,2},{4,3},{5,4},{6,5},{7,6},{8,7},{9,8},{10,9},{11,1... | collective-permute-start | bytes 13832 | tf_op jit(solution)/shard_map/ppermute | solution.py:29
  60.4 3.4 %collective-permute-start.4 = (f32[1024,128]{1,0:T(8,128)}, f32[1024,128]{1,0:T(8,128)S(1)}, u32[]{:S(2)}, u32[]{:S(2)}) collective-permute-start(f32[1024,128]{1,0:T(8,128)} %product.4), channel_id=1, source_target_pairs={{0,1},{1,0},{2,3},{3,2},{4,5},{5,4},{6,7},{7,6},{8,9},{9,8},{10,11... | collective-permute-start | bytes 1572872 | tf_op jit(solution)/shard_map/ppermute | solution.py:488
  70.2 12.7 %collective-permute-start.5 = (f32[1024,128]{1,0:T(8,128)}, f32[1024,128]{1,0:T(8,128)S(1)}, u32[]{:S(2)}, u32[]{:S(2)}) collective-permute-start(f32[1024,128]{1,0:T(8,128)} %product.5.m1_ref), channel_id=1, source_target_pairs={{0,1},{1,0},{2,3},{3,2},{4,5},{5,4},{6,7},{7,6},{8,9},{9,8},{10,11... | collective-permute-start | bytes 1572872 | tf_op jit(solution)/shard_map/ppermute | solution.py:492
  70.5 11.5 %collective-permute-start.6 = (bf16[1024,128]{1,0:T(8,128)(2,1)S(1)}, bf16[1024,128]{1,0:T(8,128)(2,1)S(1)}, u32[]{:S(2)}, u32[]{:S(2)}) collective-permute-start(bf16[1024,128]{1,0:T(8,128)(2,1)S(1)} %add_convert_fusion), channel_id=1, source_target_pairs={{2,0},{4,2},{6,4},{8,6},{10,8},{12,10},{14,12},{16,14},{18,16},{20... | collective-permute-start | bytes 786440 | tf_op jit(solution)/shard_map/ppermute | solution.py:490
  82.8 0.8 copy-start.2
